TPU v7x, 32 devices: a whole 2x2x4 slice. The times are simulated.
32 devices in a mesh: page: 8 (over z, x), band: 4 (over y, core).
Axes of the slice: x: 2, y: 2, z: 4, core: 2. Of those that a mesh axis runs over, the one named last changes fastest.
Arguments:
- hidden: bfloat16 [32768, 768], P(('page', 'band')), may hold values from -6 to 6
- page_ids: int32 [32768], P(('page', 'band')), may hold values from 0 to 1, as said below
- key_mask: int32 [32768], P(('page', 'band')), may hold values from 0 to 1, as said below
- out_grad: bfloat16 [32768, 768], P(('page', 'band')), may hold values from -6 to 6
- w_query: bfloat16 [768, 768], replicated, may hold values from -0.4375 to 0.4375
- b_query: float32 [768], replicated, may hold values from -3 to 3
- w_key: bfloat16 [768, 768], replicated, may hold values from -0.21875 to 0.21875
- w_value: bfloat16 [768, 768], replicated, may hold values from -0.21875 to 0.21875
- b_value: float32 [768], replicated, may hold values from -3 to 3
- w_out: bfloat16 [768, 768], replicated, may hold values from -0.875 to 0.875
- b_out: float32 [768], replicated, may hold values from -3 to 3
- gain_one: float32 [768], replicated, may hold values from 0.5 to 1.5
- shift_one: float32 [768], replicated, may hold values from -2 to 2
- w_up: bfloat16 [768, 3072], replicated, may hold values from -0.21875 to 0.21875
- b_up: float32 [3072], replicated, may hold values from -3 to 3
- w_down: bfloat16 [3072, 768], replicated, may hold values from -0.109375 to 0.109375
- b_down: float32 [768], replicated, may hold values from -2 to 2
- gain_two: float32 [768], replicated, may hold values from 0.5 to 1.5
- shift_two: float32 [768], replicated, may hold values from -2 to 2
Outputs:
- output: bfloat16 [32768, 768], P(('page', 'band'))
- input_grad: bfloat16 [32768, 768], P(('page', 'band'))
- grad_w_query: float32 [768, 768], replicated
- grad_b_query: float32 [768], replicated
- grad_w_key: float32 [768, 768], replicated
- grad_w_value: float32 [768, 768], replicated
- grad_b_value: float32 [768], replicated
- grad_w_out: float32 [768, 768], replicated
- grad_b_out: float32 [768], replicated
- grad_gain_one: float32 [768], replicated
- grad_shift_one: float32 [768], replicated
- grad_w_up: float32 [768, 3072], replicated
- grad_b_up: float32 [3072], replicated
- grad_w_down: float32 [3072, 768], replicated
- grad_b_down: float32 [768], replicated
- grad_gain_two: float32 [768], replicated
- grad_shift_two: float32 [768], replicated
Inputs may be any that keep to these rules, and one draw needn't show every extreme that they name: Within each block of 1024 slots the slots with key_mask 1 come first; 32768 // 1024 blocks in all, and some block is full of them in every draw. `page_ids`: document within its document group; within a block the slots with key_mask 1 are in order of document, and every document of the group has such slots in every block of the group.
All inputs are finite; a program needn't handle non-finite values.
Results may differ from a plain program's by a relative error of at most 0.015.
The roundings to bfloat16 on the way count: a program that leaves them out, or rounds other values in their place, can miss the bound.
Values may be sent and summed in bfloat16 or wider, within the bound.
No kernel may reach another device: no remote copies, remote signals or barrier semaphores. Data moves between devices by JAX's collectives and lax.ppermute only.
A program may use at most 256 MiB of HBM per device.

v0:
```python
import jax
import jax.numpy as jnp
from jax import lax
from jax.sharding import PartitionSpec as P

D = 768
HEADS = 12
HEAD = 64


def padded_2(x, sides, width):
    for axis, dim in sides:
        peers, length = (lax.axis_size(axis), x.shape[dim])
        up = [(i, (i + 1) % peers) for i in range(peers - 1)]
        down = [(j, i) for i, j in up]
        last = lax.slice_in_dim(x, length - width, length, axis=dim)
        leading = lax.slice_in_dim(x, 0, width, axis=dim)
        before = lax.ppermute(last, axis, up)
        after = lax.ppermute(leading, axis, down)
        x = jnp.concatenate([before, x, after], axis=dim)
    return x


def passed_along(block, axis, distance):
    devices = range(lax.axis_size(axis))
    route = [(i - distance, i) for i in devices if i - distance in devices]
    return lax.ppermute(block, axis, route)


def norm_rows(values, gain, shift):
    centre = jnp.mean(values, axis=-1, keepdims=True)
    centred = values - centre
    spread = jnp.mean(centred * centred, axis=-1, keepdims=True)
    return centred * lax.rsqrt(spread + 1e-12) * gain + shift


def gelu_exact(values):
    return jax.nn.gelu(values, approximate=False)


def body(
    hidden,
    page_ids,
    key_mask,
    out_grad,
    w_query,
    b_query,
    w_key,
    w_value,
    b_value,
    w_out,
    b_out,
    gain_one,
    shift_one,
    w_up,
    b_up,
    w_down,
    b_down,
    gain_two,
    shift_two,
):
    row_count = hidden.shape[0]
    pair_count = HEADS // 2
    pair_width = 2 * HEAD
    scale = HEAD ** (-0.5)
    queries = (jnp.dot(hidden, w_query, preferred_element_type=jnp.float32) + b_query).astype(
        jnp.bfloat16
    )
    key_rows = jnp.dot(hidden, w_key, preferred_element_type=jnp.float32).astype(jnp.bfloat16)
    value_rows = (jnp.dot(hidden, w_value, preferred_element_type=jnp.float32) + b_value).astype(
        jnp.bfloat16
    )
    key_tags = jnp.where(key_mask == 1, page_ids + 1, 0)
    near_pack, near_tags = (
        padded_2(jnp.concatenate([key_rows, value_rows], axis=1), (("band", 0),), row_count),
        padded_2(key_tags, (("band", 0),), row_count),
    )
    allowed = page_ids[:, None] + 1 == near_tags[None, :]

    def to_pairs(matrix):
        return matrix.reshape(matrix.shape[0], pair_count, pair_width).transpose(1, 0, 2)

    def from_pairs(stacked):
        return stacked.transpose(1, 0, 2).reshape(stacked.shape[1], pair_count * pair_width)

    query_pairs = to_pairs(queries)
    key_pairs = to_pairs(near_pack[:, :D])
    value_pairs = to_pairs(near_pack[:, D:])

    def pair_scores(query_pair, key_pair):
        scores = (
            jnp.einsum(
                "ihd,jhd->hij",
                query_pair.reshape(-1, 2, HEAD),
                key_pair.reshape(-1, 2, HEAD),
                preferred_element_type=jnp.float32,
            )
            * scale
        )
        return jnp.where(allowed[None], scores, -1e30)

    def pair_forward(items):
        query_pair, key_pair, value_pair = items
        scores = pair_scores(query_pair, key_pair)
        row_top = jnp.max(scores, axis=2, keepdims=True)
        weights = jnp.exp(scores - row_top)
        row_total = jnp.sum(weights, axis=2, keepdims=True)
        probs_low = (weights / row_total).astype(jnp.bfloat16)
        mixed_part = jnp.einsum(
            "hij,jhd->ihd",
            probs_low,
            value_pair.reshape(-1, 2, HEAD),
            preferred_element_type=jnp.float32,
        )
        logsum = row_top[:, :, 0] + jnp.log(row_total[:, :, 0])
        return (mixed_part.reshape(-1, pair_width).astype(jnp.bfloat16), logsum)

    mixed_pairs, logsums = lax.map(pair_forward, (query_pairs, key_pairs, value_pairs))
    mixed = from_pairs(mixed_pairs)
    attention = jnp.dot(mixed, w_out, preferred_element_type=jnp.float32) + b_out
    resid_one = hidden.astype(jnp.float32) + attention
    normed_one = norm_rows(resid_one, gain_one, shift_one)
    normed_low = normed_one.astype(jnp.bfloat16)
    upper_in = jnp.dot(normed_low, w_up, preferred_element_type=jnp.float32) + b_up
    active = gelu_exact(upper_in).astype(jnp.bfloat16)
    branch = jnp.dot(active, w_down, preferred_element_type=jnp.float32) + b_down
    resid_two = normed_one + branch
    result = norm_rows(resid_two, gain_two, shift_two)
    cotangent = out_grad.astype(jnp.float32) * key_mask.astype(jnp.float32)[:, None]
    unused_two, norm_back_two = jax.vjp(norm_rows, resid_two, gain_two, shift_two)
    d_resid_two, grad_gain_two, grad_shift_two = norm_back_two(cotangent)
    d_branch = d_resid_two.astype(jnp.bfloat16)
    grad_w_down = jnp.einsum("rf,rd->fd", active, d_branch, preferred_element_type=jnp.float32)
    grad_b_down = jnp.sum(d_branch.astype(jnp.float32), axis=0)
    d_active = jnp.einsum("rd,fd->rf", d_branch, w_down, preferred_element_type=jnp.float32)
    unused_gelu, gelu_back = jax.vjp(gelu_exact, upper_in)
    d_upper = gelu_back(d_active)[0].astype(jnp.bfloat16)
    grad_w_up = jnp.einsum("rd,rf->df", normed_low, d_upper, preferred_element_type=jnp.float32)
    grad_b_up = jnp.sum(d_upper.astype(jnp.float32), axis=0)
    d_normed = (
        jnp.einsum("rf,df->rd", d_upper, w_up, preferred_element_type=jnp.float32) + d_resid_two
    )
    unused_one, norm_back_one = jax.vjp(norm_rows, resid_one, gain_one, shift_one)
    d_resid_one, grad_gain_one, grad_shift_one = norm_back_one(d_normed)
    d_attention = d_resid_one.astype(jnp.bfloat16)
    grad_w_out = jnp.einsum("rd,re->de", mixed, d_attention, preferred_element_type=jnp.float32)
    grad_b_out = jnp.sum(d_attention.astype(jnp.float32), axis=0)
    d_mixed = jnp.einsum(
        "re,de->rd", d_attention, w_out, preferred_element_type=jnp.float32
    ).astype(jnp.bfloat16)

    def pair_backward(items):
        query_pair, key_pair, value_pair, grad_pair, logsum = items
        scores = pair_scores(query_pair, key_pair)
        probs = jnp.exp(scores - logsum[:, :, None])
        probs_low = probs.astype(jnp.bfloat16)
        query_heads = query_pair.reshape(-1, 2, HEAD)
        key_heads = key_pair.reshape(-1, 2, HEAD)
        grad_heads = grad_pair.reshape(-1, 2, HEAD)
        grad_probs = jnp.einsum(
            "ihd,jhd->hij",
            grad_heads,
            value_pair.reshape(-1, 2, HEAD),
            preferred_element_type=jnp.float32,
        )
        inner_sum = jnp.sum(probs * grad_probs, axis=2, keepdims=True)
        grad_scores = (probs * (grad_probs - inner_sum)).astype(jnp.bfloat16)
        grad_query = (
            jnp.einsum("hij,jhd->ihd", grad_scores, key_heads, preferred_element_type=jnp.float32)
            * scale
        )
        grad_key = (
            jnp.einsum("hij,ihd->jhd", grad_scores, query_heads, preferred_element_type=jnp.float32)
            * scale
        )
        grad_value = jnp.einsum(
            "hij,ihd->jhd", probs_low, grad_heads, preferred_element_type=jnp.float32
        )
        return (
            grad_query.reshape(-1, pair_width),
            grad_key.reshape(-1, pair_width),
            grad_value.reshape(-1, pair_width),
        )

    dq_pairs, dk_pairs, dv_pairs = lax.map(
        pair_backward, (query_pairs, key_pairs, value_pairs, to_pairs(d_mixed), logsums)
    )
    d_queries = from_pairs(dq_pairs).astype(jnp.bfloat16)
    d_near = jnp.concatenate([from_pairs(dk_pairs), from_pairs(dv_pairs)], axis=1)
    from_above = passed_along(d_near[:row_count].astype(jnp.bfloat16), "band", -1).astype(
        jnp.float32
    )
    from_below = passed_along(d_near[2 * row_count :].astype(jnp.bfloat16), "band", 1).astype(
        jnp.float32
    )
    d_pack = (d_near[row_count : 2 * row_count] + from_above + from_below).astype(jnp.bfloat16)
    d_keys = d_pack[:, :D]
    d_values = d_pack[:, D:]
    grad_w_query = jnp.einsum("rd,re->de", hidden, d_queries, preferred_element_type=jnp.float32)
    grad_b_query = jnp.sum(d_queries.astype(jnp.float32), axis=0)
    grad_w_key = jnp.einsum("rd,re->de", hidden, d_keys, preferred_element_type=jnp.float32)
    grad_w_value = jnp.einsum("rd,re->de", hidden, d_values, preferred_element_type=jnp.float32)
    grad_b_value = jnp.sum(d_values.astype(jnp.float32), axis=0)
    input_sum = jnp.einsum("re,de->rd", d_queries, w_query, preferred_element_type=jnp.float32)
    input_sum = input_sum + jnp.einsum(
        "re,de->rd", d_keys, w_key, preferred_element_type=jnp.float32
    )
    input_sum = input_sum + jnp.einsum(
        "re,de->rd", d_values, w_value, preferred_element_type=jnp.float32
    )
    input_grad = (input_sum + d_resid_one).astype(jnp.bfloat16)
    grads = (
        grad_w_query,
        grad_b_query,
        grad_w_key,
        grad_w_value,
        grad_b_value,
        grad_w_out,
        grad_b_out,
        grad_gain_one,
        grad_shift_one,
        grad_w_up,
        grad_b_up,
        grad_w_down,
        grad_b_down,
        grad_gain_two,
        grad_shift_two,
    )
    flat_grads = jnp.concatenate([member.reshape(-1) for member in grads])
    total_len = flat_grads.shape[0]
    devices = lax.axis_size("page") * lax.axis_size("band")
    line_count = -(-total_len // 128)
    per_device = -(-line_count // devices)
    line_count = per_device * devices
    lined = jnp.pad(flat_grads, (0, line_count * 128 - total_len)).reshape(per_device, devices, 128)
    padded = lined.transpose(1, 0, 2).reshape(line_count, 128)
    shares = lax.psum_scatter(padded, ("page", "band"), scatter_dimension=0, tiled=True)
    summed = lax.all_gather(
        shares.astype(jnp.bfloat16), ("page", "band"), axis=0, tiled=True
    ).astype(shares.dtype)
    summed = summed.reshape(devices, per_device, 128).transpose(1, 0, 2).reshape(-1)[:total_len]
    reduced = []
    offset = 0
    for member in grads:
        length = member.size
        reduced.append(summed[offset : offset + length].reshape(member.shape))
        offset = offset + length
    return (
        result.astype(jnp.bfloat16),
        input_grad,
        reduced[0],
        reduced[1],
        reduced[2],
        reduced[3],
        reduced[4],
        reduced[5],
        reduced[6],
        reduced[7],
        reduced[8],
        reduced[9],
        reduced[10],
        reduced[11],
        reduced[12],
        reduced[13],
        reduced[14],
    )


def solution(mesh):
    placed = (
        P(("page", "band"), None),
        P(("page", "band")),
        P(("page", "band")),
        P(("page", "band"), None),
        P(),
        P(),
        P(),
        P(),
        P(),
        P(),
        P(),
        P(),
        P(),
        P(),
        P(),
        P(),
        P(),
        P(),
        P(),
    )
    return jax.shard_map(
        body,
        mesh=mesh,
        in_specs=placed,
        out_specs=(
            P(("page", "band"), None),
            P(("page", "band"), None),
            P(),
            P(),
            P(),
            P(),
            P(),
            P(),
            P(),
            P(),
            P(),
            P(),
            P(),
            P(),
            P(),
            P(),
            P(),
        ),
        check_vma=False,
    )
```

profile of v0, /device:TPU:0, one launch (start us, length us, event | category | flops | bytes accessed | tf_op | source)
XLA Modules:
  0.0 1850.9 jit_solution(1519786430209476050)
XLA Ops:
  32.9 17.7 pad_maximum_fusion.1
  58.8 247.9 %while.28 = (s32[]{:T(128)}, bf16[6,1024,128]{1,2,0:T(8,128)(2,1)}, f32[6,2,1024]{2,1,0:T(2,128)}, bf16[6,3072,128]{1,2,0:T(8,128)(2,1)}, bf16[6,1024,128]{1,2,0...) while((s32[]{:T(128)}, bf16[6,1024,128]{1,2,0:T(8,128)(2,1)}, ...), condition=%wide.region_3.4_spmd.clone, body=%wide.region_0.3_spmd.clone.sunk | while | flops 1689384960 | bytes 94454880 | solution.py:118
  63.4 11.2 fusion.120
  74.6 11.8 fusion.121
  87.1 12.5 fusion.122
  104.7 11.2 fusion.120
  115.9 11.8 fusion.121
  128.3 12.5 fusion.122
  146.0 11.2 fusion.120
  157.2 11.8 fusion.121
  169.6 12.5 fusion.122
  187.3 11.2 fusion.120
  198.4 11.8 fusion.121
  210.9 12.5 fusion.122
  228.5 11.2 fusion.120
  239.7 11.8 fusion.121
  252.2 12.5 fusion.122
  269.8 11.2 fusion.120
  281.0 11.8 fusion.121
  293.4 12.5 fusion.122
  311.3 48.9 %multiply_convert_fusion.1 = (bf16[1024,3072]{1,0:T(8,128)(2,1)S(1)}, f32[1024,3072]{1,0:T(8,128)}, f32[1024,3072]{1,0:T(8,128)}) fusion(f32[3072]{0:T(1024)S(1)} %copy-done.46, bf16[768,3072]{1,0:T(8,128)(2,1)S(1)} %bitcast.190, f32[1024,768]{0,1:T(8,128)S(1)} %get-tuple-element.314, f32[768]{0:T(1024)S(1)} %copy-done.51, f32[768]{0:T(1024)S(1)} %copy-done.36, ...), kind=kOutput, calls=%fused_computation.45 | convolution fusion | flops 5043388416 | bytes 39348224 | tf_op jit(solution)/shard_map/dot_general | solution.py:124
  373.8 19.1 %convert_reduce_fusion = (f32[3072]{0:T(1024)}, bf16[1024,3072]{1,0:T(8,128)(2,1)}) fusion(f32[1024,3072]{1,0:T(8,128)} %get-tuple-element.281, bf16[1024,768]{0,1:T(8,128)(2,1)} %get-tuple-element.275, bf16[3072,768]{1,0:T(8,128)(2,1)} %param.38, f32[1024,3072]{1,0:T(8,128)} %get-tuple-element.315, f32[3072]{0:T(1024)S(1)} %copy-done.46), kind=kOutput, calls=%fused_computation.43 | convolution fusion | flops 4885312512 | bytes 37773312 | tf_op jit(solution)/shard_map/rd,fd->rf/dot_general | solution.py:135
  392.9 11.5 multiply_reduce_fusion.2
  411.8 507.8 %while.29 = (s32[]{:T(128)}, bf16[6,1024,128]{1,2,0:T(8,128)(2,1)}, f32[6,3072,128]{1,2,0:T(8,128)}, f32[6,3072,128]{1,2,0:T(8,128)}, bf16[6,3072,128]{1,2,0:T(8...) while((s32[]{:T(128)}, bf16[6,1024,128]{1,2,0:T(8,128)(2,1)}, ...), condition=%wide.region_14.15_spmd.clone, body=%wide.region_12.14_spmd.clone.sunk | while | flops 4124702720 | bytes 282141888 | solution.py:185
  414.4 10.1 fusion.133
  431.0 19.9 %multiply_reduce_fusion.8 = (f32[2,1024]{1,0:T(2,128)S(1)}, f32[2,1024,3072]{2,1,0:T(8,128)}) fusion(f32[2,1024,3072]{2,1,0:T(8,128)} %fusion.133, f32[2,1024]{1,0:T(2,128)S(1)} %dynamic-slice_bitcast_fusion.2, pred[1024,3072]{1,0:T(8,128)(4,1)} %broadcast_compare_fusion.5, bf16[1024,2,64]{0,2,1:T(8,128)(2,1)S(1)} %bitcast.178, ...), kind=kOutput, calls=%fused_computation.18.clone.1 | convolution fusion | flops 836761600 | bytes 54542336 | tf_op jit(solution)/shard_map/while/body/eval_jaxpr/ihd,jhd->hij/dot_general | solution.py:160
  450.9 17.8 multiply_convert_fusion.3
  474.0 11.5 fusion.134
  498.9 10.1 fusion.133
  515.6 19.9 %multiply_reduce_fusion.8 = (f32[2,1024]{1,0:T(2,128)S(1)}, f32[2,1024,3072]{2,1,0:T(8,128)}) fusion(f32[2,1024,3072]{2,1,0:T(8,128)} %fusion.133, f32[2,1024]{1,0:T(2,128)S(1)} %dynamic-slice_bitcast_fusion.2, pred[1024,3072]{1,0:T(8,128)(4,1)} %broadcast_compare_fusion.5, bf16[1024,2,64]{0,2,1:T(8,128)(2,1)S(1)} %bitcast.178, ...), kind=kOutput, calls=%fused_computation.18.clone.1 | convolution fusion | flops 836761600 | bytes 54542336 | tf_op jit(solution)/shard_map/while/body/eval_jaxpr/ihd,jhd->hij/dot_general | solution.py:160
  535.5 17.8 multiply_convert_fusion.3
  558.5 11.5 fusion.134
  583.5 10.1 fusion.133
  600.1 19.9 %multiply_reduce_fusion.8 = (f32[2,1024]{1,0:T(2,128)S(1)}, f32[2,1024,3072]{2,1,0:T(8,128)}) fusion(f32[2,1024,3072]{2,1,0:T(8,128)} %fusion.133, f32[2,1024]{1,0:T(2,128)S(1)} %dynamic-slice_bitcast_fusion.2, pred[1024,3072]{1,0:T(8,128)(4,1)} %broadcast_compare_fusion.5, bf16[1024,2,64]{0,2,1:T(8,128)(2,1)S(1)} %bitcast.178, ...), kind=kOutput, calls=%fused_computation.18.clone.1 | convolution fusion | flops 836761600 | bytes 54542336 | tf_op jit(solution)/shard_map/while/body/eval_jaxpr/ihd,jhd->hij/dot_general | solution.py:160
  620.0 17.8 multiply_convert_fusion.3
  643.1 11.5 fusion.134
  668.0 10.1 fusion.133
  684.6 19.9 %multiply_reduce_fusion.8 = (f32[2,1024]{1,0:T(2,128)S(1)}, f32[2,1024,3072]{2,1,0:T(8,128)}) fusion(f32[2,1024,3072]{2,1,0:T(8,128)} %fusion.133, f32[2,1024]{1,0:T(2,128)S(1)} %dynamic-slice_bitcast_fusion.2, pred[1024,3072]{1,0:T(8,128)(4,1)} %broadcast_compare_fusion.5, bf16[1024,2,64]{0,2,1:T(8,128)(2,1)S(1)} %bitcast.178, ...), kind=kOutput, calls=%fused_computation.18.clone.1 | convolution fusion | flops 836761600 | bytes 54542336 | tf_op jit(solution)/shard_map/while/body/eval_jaxpr/ihd,jhd->hij/dot_general | solution.py:160
  704.5 17.8 multiply_convert_fusion.3
  727.6 11.5 fusion.134
  752.5 10.1 fusion.133
  769.1 19.9 %multiply_reduce_fusion.8 = (f32[2,1024]{1,0:T(2,128)S(1)}, f32[2,1024,3072]{2,1,0:T(8,128)}) fusion(f32[2,1024,3072]{2,1,0:T(8,128)} %fusion.133, f32[2,1024]{1,0:T(2,128)S(1)} %dynamic-slice_bitcast_fusion.2, pred[1024,3072]{1,0:T(8,128)(4,1)} %broadcast_compare_fusion.5, bf16[1024,2,64]{0,2,1:T(8,128)(2,1)S(1)} %bitcast.178, ...), kind=kOutput, calls=%fused_computation.18.clone.1 | convolution fusion | flops 836761600 | bytes 54542336 | tf_op jit(solution)/shard_map/while/body/eval_jaxpr/ihd,jhd->hij/dot_general | solution.py:160
  789.0 17.8 multiply_convert_fusion.3
  812.1 11.5 fusion.134
  837.1 10.1 fusion.133
  853.7 19.9 %multiply_reduce_fusion.8 = (f32[2,1024]{1,0:T(2,128)S(1)}, f32[2,1024,3072]{2,1,0:T(8,128)}) fusion(f32[2,1024,3072]{2,1,0:T(8,128)} %fusion.133, f32[2,1024]{1,0:T(2,128)S(1)} %dynamic-slice_bitcast_fusion.2, pred[1024,3072]{1,0:T(8,128)(4,1)} %broadcast_compare_fusion.5, bf16[1024,2,64]{0,2,1:T(8,128)(2,1)S(1)} %bitcast.178, ...), kind=kOutput, calls=%fused_computation.18.clone.1 | convolution fusion | flops 836761600 | bytes 54542336 | tf_op jit(solution)/shard_map/while/body/eval_jaxpr/ihd,jhd->hij/dot_general | solution.py:160
  873.6 17.8 multiply_convert_fusion.3
  896.7 11.5 fusion.134
  943.6 29.6 %collective-permute-start.5 = (bf16[1024,1536]{0,1:T(8,128)(2,1)}, bf16[1024,1536]{0,1:T(8,128)(2,1)}, u32[]{:S(2)}, u32[]{:S(2)}) collective-permute-start(bf16[1024,1536]{0,1:T(8,128)(2,1)} %get-tuple-element.304), channel_id=1, source_target_pairs={{0,1},{1,2},{2,3},{4,5},{5,6},{6,7},{8,9},{9,10},{10,11},{12,13},{... | collective-permute-start | bytes 9437192 | tf_op jit(solution)/shard_map/ppermute | solution.py:27
  990.0 10.3 fusion.55
  1000.2 10.7 reshape.264
  1037.8 21.3 %dynamic-update-slice.2 = f32[7087104]{0:T(1024)} dynamic-update-slice(f32[7087104]{0:T(1024)} %constant_dynamic-update-slice_fusion.12, f32[589824]{0:T(1024)} %reshape.260, s32[]{} %constant.141) | dynamic-update-slice | bytes 4718596
  1059.1 21.3 %dynamic-update-slice.3 = f32[7087104]{0:T(1024)} dynamic-update-slice(f32[7087104]{0:T(1024)} %dynamic-update-slice.2, f32[589824]{0:T(1024)} %reshape.261, s32[]{} %constant.142) | dynamic-update-slice | bytes 4718596
  1081.7 20.2 %dynamic-update-slice.5 = f32[7087104]{0:T(1024)} dynamic-update-slice(f32[7087104]{0:T(1024)} %constant_dynamic-update-slice_fusion.11, f32[589824]{0:T(1024)S(1)} %reshape.262, s32[]{} %constant.144) | dynamic-update-slice | bytes 4718596
  1105.9 80.4 %dynamic-update-slice.9 = f32[7087104]{0:T(1024)} dynamic-update-slice(f32[7087104]{0:T(1024)} %constant_dynamic-update-slice_fusion.8, f32[2359296]{0:T(1024)} %bitcast.175, s32[]{} %constant.148) | dynamic-update-slice | bytes 18874372
  1187.6 80.5 %dynamic-update-slice.11 = f32[7087104]{0:T(1024)} dynamic-update-slice(f32[7087104]{0:T(1024)} %constant_dynamic-update-slice_fusion.7, f32[2359296]{0:T(1024)} %reshape.264, s32[]{} %constant.150) | dynamic-update-slice | bytes 18874372
  1272.0 10.4 pad.4
  1282.4 18.8 %copy.80 = f32[32,1731,128]{2,1,0:T(8,128)} copy(f32[32,1731,128]{2,0,1:T(8,128)S(1)} %bitcast.164) | data formatting | bytes 56721408 | tf_op jit(solution)/shard_map/transpose | solution.py:236
  1301.2 25.3 %reshape.266 = f32[55392,128]{1,0:T(8,128)} reshape(f32[32,1731,128]{2,1,0:T(8,128)} %copy.80) | data formatting | bytes 56721408 | tf_op jit(solution)/shard_map/reshape | solution.py:236
  1326.5 302.6 %fusion.4 = f32[1744,128]{1,0:T(8,128)S(1)} fusion(f32[55392,128]{1,0:T(8,128)} %reshape.266), kind=kCustom, calls=%all-reduce-scatter | all-reduce-scatter fusion | flops 7143425 | bytes 29253632
  1646.6 100.6 %all-gather.3.cloned.1.call-done = bf16[32,1731,128]{2,1,0:T(8,128)(2,1)} async-done(((bf16[1,1731,128]{2,1,0:T(8,128)(2,1)}), bf16[32,1731,128]{2,1,0:T(8,128)(2,1)}) %all-gather.3.cloned.1.call-update) | async-done | bytes 14180368 | tf_op jit(solution)/shard_map/all_gather | solution.py:238
  1747.2 25.4 %copy_convert_fusion = (f32[32,1731,128]{2,0,1:T(8,128)}, f32[1731,32,128]{2,1,0:T(8,128)}) fusion(bf16[32,1731,128]{2,1,0:T(8,128)(2,1)} %all-gather.3.cloned.1.call-done), kind=kLoop, calls=%fused_computation.41 | loop fusion | flops 7090176 | bytes 70901760 | tf_op jit(solution)/shard_map/transpose | solution.py:241
  1772.6 31.3 %slice.104 = f32[9232,768]{1,0:T(8,128)} reshape(f32[1731,32,128]{2,1,0:T(8,128)} %get-tuple-element.302) | data formatting | bytes 56721408 | tf_op jit(solution)/shard_map/slice | solution.py:246
  1831.1 11.0 reshape.269
  (316 shorter events, 368.7 us)
Async XLA Ops:
  7.2 299.5 %copy-start = (bf16[768,768]{1,0:T(8,128)(2,1)S(1)}, bf16[768,768]{1,0:T(8,128)(2,1)}, u32[]{:S(2)}) copy-start(bf16[768,768]{1,0:T(8,128)(2,1)} %param.32) | copy-start | bytes 3538948
  7.2 3.4 copy-start.47
  7.2 1740.0 %all-gather.3.cloned.1.call-start = ((), (), s32[]{:S(2)}) async-start(), calls=%async_computation | async-start | bytes 14665728 | tf_op jit(solution)/shard_map/all_gather | solution.py:238
  7.3 3.4 copy-start.13
  7.3 3.4 copy-start.18
  12.1 7.5 copy-start.38
  12.1 7.5 copy-start.39
  12.2 12.9 copy-start.43
  12.2 12.9 copy-start.48
  14.3 18.5 %collective-permute-start = (bf16[1024,1536]{0,1:T(8,128)(2,1)}, bf16[1024,1536]{0,1:T(8,128)(2,1)}, u32[]{:S(2)}, u32[]{:S(2)}) collective-permute-start(bf16[1024,1536]{0,1:T(8,128)(2,1)} %pad_maximum_fusion.2), channel_id=1, source_target_pairs={{0,1},{1,2},{2,3},{4,5},{5,6},{6,7},{8,9},{9,10},{10,11},{12,13},{... | collective-permute-start | bytes 9437192 | tf_op jit(solution)/shard_map/ppermute | solution.py:18
  18.3 14.5 collective-permute-start.1
  20.2 12.6 collective-permute-start.2
  23.7 9.1 collective-permute-start.3
  58.8 247.9 %copy-start.49 = (f32[768]{0:T(1024)S(1)}, f32[768]{0:T(1024)}, u32[]{:S(2)}) copy-start(f32[768]{0:T(1024)} %param.33) | copy-start | bytes 9220
  306.7 3.7 copy-start.16
  306.7 3.7 copy-start.20
  306.7 4.2 slice-start.2
  306.7 4.2 slice-start.3
  306.7 53.5 %slice-start = ((s8[4718592]{0:T(1024)(128)(4,1)}), s8[4194304]{0:T(1024)(128)(4,1)S(1)}, s32[]{:S(2)}) async-start(s8[4718592]{0:T(1024)(128)(4,1)} %bitcast.187), calls=%async_computation.1 | async-start | bytes 8388608
  310.4 49.7 %copy-start.9 = (f32[1024,768]{0,1:T(8,128)}, f32[1024,768]{0,1:T(8,128)S(1)}, u32[]{:S(2)}) copy-start(f32[1024,768]{0,1:T(8,128)S(1)} %get-tuple-element.314) | copy-start | bytes 9437188
  310.5 93.9 %copy-start.25 = (f32[1024]{0:T(1024)}, f32[1024]{0:T(1024)S(1)}, u32[]{:S(2)}) copy-start(f32[1024]{0:T(1024)S(1)} %broadcast_multiply_fusion.1) | copy-start | bytes 12292
  311.3 93.1 %copy-start.30 = (f32[1024]{0:T(1024)}, f32[1024]{0:T(1024)S(1)}, u32[]{:S(2)}) copy-start(f32[1024]{0:T(1024)S(1)} %fusion.38) | copy-start | bytes 12292
  311.3 48.9 %slice-start.1 = ((s8[4718592]{0:T(1024)(128)(4,1)}), s8[524288]{0:T(1024)(128)(4,1)S(1)}, s32[]{:S(2)}) async-start(s8[4718592]{0:T(1024)(128)(4,1)} %bitcast.187), calls=%async_computation.2 | async-start | bytes 1048576
  311.3 48.9 %copy-start.50 = (f32[768]{0:T(1024)S(1)}, f32[768]{0:T(1024)}, u32[]{:S(2)}) copy-start(f32[768]{0:T(1024)} %param.39) | copy-start | bytes 9220
  360.1 6.1 copy-start.53
  360.2 6.0 copy-start.6
  360.2 6.0 copy-start.22
  360.2 6.0 copy-start.27
  392.9 11.5 copy-start.10
  405.2 3.8 copy-start.4
  405.2 3.8 copy-start.23
  468.7 5.3 copy-start.2
  468.7 5.3 copy-start.3
  553.2 5.3 copy-start.2
  553.2 5.3 copy-start.3
  637.8 5.3 copy-start.2
  637.8 5.3 copy-start.3
  722.3 5.3 copy-start.2
  722.3 5.3 copy-start.3
  806.8 5.3 copy-start.2
  806.8 5.3 copy-start.3
  891.4 5.3 copy-start.2
  891.4 5.3 copy-start.3
  942.2 33.4 %copy-start.26 = (f32[1024]{0:T(1024)S(1)}, f32[1024]{0:T(1024)}, u32[]{:S(2)}) copy-start(f32[1024]{0:T(1024)} %copy-done.25) | copy-start | bytes 12292
  942.2 33.4 %copy-start.31 = (f32[1024]{0:T(1024)S(1)}, f32[1024]{0:T(1024)}, u32[]{:S(2)}) copy-start(f32[1024]{0:T(1024)} %copy-done.30) | copy-start | bytes 12292
  942.2 33.4 %copy-start.37 = (f32[768]{0:T(1024)S(1)}, f32[768]{0:T(1024)}, u32[]{:S(2)}) copy-start(f32[768]{0:T(1024)} %param.34) | copy-start | bytes 9220
  942.2 33.4 %copy-start.52 = (f32[768]{0:T(1024)S(1)}, f32[768]{0:T(1024)}, u32[]{:S(2)}) copy-start(f32[768]{0:T(1024)} %param.35) | copy-start | bytes 9220
  942.2 71.7 %collective-permute-start.4 = (bf16[1024,1536]{0,1:T(8,128)(2,1)}, bf16[1024,1536]{0,1:T(8,128)(2,1)}, u32[]{:S(2)}, u32[]{:S(2)}) collective-permute-start(bf16[1024,1536]{0,1:T(8,128)(2,1)} %get-tuple-element.303), channel_id=1, source_target_pairs={{1,0},{2,1},{3,2},{5,4},{6,5},{7,6},{9,8},{10,9},{11,10},{13,12},{... | collective-permute-start | bytes 9437192 | tf_op jit(solution)/shard_map/ppermute | solution.py:27
  943.6 70.3 %collective-permute-start.5 = (bf16[1024,1536]{0,1:T(8,128)(2,1)}, bf16[1024,1536]{0,1:T(8,128)(2,1)}, u32[]{:S(2)}, u32[]{:S(2)}) collective-permute-start(bf16[1024,1536]{0,1:T(8,128)(2,1)} %get-tuple-element.304), channel_id=1, source_target_pairs={{0,1},{1,2},{2,3},{4,5},{5,6},{6,7},{8,9},{9,10},{10,11},{12,13},{... | collective-permute-start | bytes 9437192 | tf_op jit(solution)/shard_map/ppermute | solution.py:27
  984.0 6.0 copy-start.15
  1013.9 5.5 copy-start.14
  1019.4 5.6 copy-start.7
  1080.4 21.6 %copy-start.32 = (f32[768]{0:T(1024)S(1)}, f32[768]{0:T(1024)}, u32[]{:S(2)}) copy-start(f32[768]{0:T(1024)} %get-tuple-element.276) | copy-start | bytes 9220
  1080.4 22.9 %copy-start.41 = (f32[768]{0:T(1024)S(1)}, f32[768]{0:T(1024)}, u32[]{:S(2)}) copy-start(f32[768]{0:T(1024)} %get-tuple-element.228) | copy-start | bytes 9220
  1080.4 24.2 %copy-start.40 = (f32[768]{0:T(1024)S(1)}, f32[768]{0:T(1024)}, u32[]{:S(2)}) copy-start(f32[768]{0:T(1024)} %get-tuple-element.234) | copy-start | bytes 9220
  1105.9 80.4 %copy-start.34 = (f32[3072]{0:T(1024)S(1)}, f32[3072]{0:T(1024)}, u32[]{:S(2)}) copy-start(f32[3072]{0:T(1024)} %get-tuple-element.319) | copy-start | bytes 36868
  1187.6 80.5 %copy-start.29 = (f32[768]{0:T(1024)S(1)}, f32[768]{0:T(1024)}, u32[]{:S(2)}) copy-start(f32[768]{0:T(1024)} %get-tuple-element.274) | copy-start | bytes 9220
  1187.6 81.8 %copy-start.33 = (f32[768]{0:T(1024)S(1)}, f32[768]{0:T(1024)}, u32[]{:S(2)}) copy-start(f32[768]{0:T(1024)} %get-tuple-element.230) | copy-start | bytes 9220
  1187.6 83.1 %copy-start.28 = (f32[768]{0:T(1024)S(1)}, f32[768]{0:T(1024)}, u32[]{:S(2)}) copy-start(f32[768]{0:T(1024)} %get-tuple-element.235) | copy-start | bytes 9220
  1629.1 7.5 copy-start.12
  1629.2 5.1 collective-permute-start.6
  1638.2 3.0 copy-start.8
  1638.2 3.0 copy-start.45
  1831.1 12.6 copy-start.1
  (12 other events, 23.6 us)
Sparse Core Ops, SparseCore 0:
  1636.8 110.3 all-gather.2
where the time goes:
time: 1880 us; the launch traced here: 1850 us
  matrix products  593 us (32%)
  local copies, waits for them, and re-layouts  507 us (27%)
  blocking collectives  303 us (16%)
  other arithmetic  286 us (15%)
  waiting for transfers between devices  102 us (5%)
  starting transfers between devices  45.3 us (2%)
    unnamed x1, blocking collectives  303 us
    unnamed x134, local copies, waits for them, and re-layouts  255 us
    dot_general x12, matrix products, pair_scores(): jnp.einsum('ihd,jhd->hij', query_pair.reshape(-1, 2, HEAD), key_pair.resh...  128 us
    dot_general x6, matrix products, pair_backward(): jnp.einsum('ihd,jhd->hij', grad_heads, value_pair.reshape(-1, 2, HEAD), p...  119 us
    convert_element_type x6, other arithmetic, pair_backward(): grad_scores = (probs * (grad_probs - inner_sum)).astype(jnp.bfloat16)  107 us
    all_gather x1, waiting for transfers between devices, body(): lax.all_gather(shares.astype(jnp.bfloat16), ('page', 'band'), axis=0, til...  101 us
    dot_general x6, matrix products, pair_forward(): jnp.einsum('hij,jhd->ihd', probs_low, value_pair.reshape(-1, 2, HEAD), pr...  75 us
    reduce_sum x6, other arithmetic, pair_forward(): row_total = jnp.sum(weights, axis=2, keepdims=True)  71 us
  transfers between devices with their start and end apart: 8, of which 2 were waited for; matrix products, arithmetic and copies ran while one was open for 3% of the time, Pallas kernels for 0%

commit v1 on v0

v1 whole, which is shorter than its diff:
```python
import functools

import jax
import jax.numpy as jnp
from jax import lax
from jax.experimental import pallas as pl
from jax.experimental.pallas import tpu as pltpu
from jax.sharding import PartitionSpec as P


HEAD = 64
PAIR = 128
BLOCKED = -1e30
SAFE = 60.0
NT = (((1,), (1,)), ((), ()))
NN = (((1,), (0,)), ((), ()))
TN = (((0,), (0,)), ((), ()))
F32 = jnp.float32
BF16 = jnp.bfloat16
SCALE = HEAD**-0.5
TILE = 256


def mm(a, b, dims):
    return lax.dot_general(a, b, dims, preferred_element_type=F32)


def col_sum(x):
    return jnp.sum(x, axis=0, keepdims=True)


def tile_at(i, tile=TILE):
    return pl.ds(pl.multiple_of(i * tile, tile), tile)


def parts(x):
    hi = x.astype(BF16)
    rest = x - hi.astype(F32)
    mid = rest.astype(BF16)
    return hi, mid, (rest - mid.astype(F32)).astype(BF16)


def same_half():
    a, b = (lax.broadcasted_iota(jnp.int32, (PAIR, PAIR), i) < HEAD for i in (0, 1))
    return jnp.where(a == b, 1.0, 0.0).astype(BF16)


def left_lanes():
    return lax.broadcasted_iota(jnp.int32, (1, PAIR), 1) < HEAD


def attend_kernel(keys, q_ref, k_ref, v_ref, qtag_ref, ktag_ref, o_ref, ext_ref, qx0, qx1, vt, acc0, acc1, top0, top1):
    rows, near = q_ref.shape[0], k_ref.shape[0]
    left = left_lanes()
    q_pair = q_ref[...] * jnp.asarray(SCALE, BF16)
    zero = jnp.zeros_like(q_pair)
    qx0[:, :PAIR] = jnp.where(left, q_pair, zero)
    qx1[:, :PAIR] = jnp.where(left, zero, q_pair)
    qx0[:, PAIR:] = qtag_ref[...]
    qx1[:, PAIR:] = qtag_ref[...]
    turned = v_ref[...].T
    vt[:HEAD, :] = turned[:HEAD]
    vt[HEAD:PAIR, :] = jnp.ones((HEAD, near), BF16)
    vt[PAIR:, :] = turned[HEAD:]
    heads = ((acc0, top0, qx0, slice(0, PAIR)), (acc1, top1, qx1, slice(HEAD, HEAD + PAIR)))
    for acc, *_ in heads:
        acc[...] = jnp.zeros_like(acc)
    halves = same_half()

    def longest(x):
        x = x.astype(F32)
        return jnp.max(mm((x * x).astype(BF16), halves, NN), axis=0, keepdims=True)

    plain = jnp.max(longest(k_ref[...]) * longest(q_pair)) < (SAFE * 0.98) ** 2
    key_side = lambda ks: jnp.concatenate([k_ref[ks, :], ktag_ref[ks, :]], axis=1)

    @pl.when(plain)
    def _():
        for _, top, *_ in heads:
            top[...] = jnp.zeros_like(top)
        for band in range(near // rows):
            for n in range(1, rows // TILE + 1):
                @pl.when(keys[band] == n)
                def _():
                    ks = pl.ds(band * rows, n * TILE)
                    kx = key_side(ks)
                    for acc, _, qx, at in heads:
                        p = jnp.exp(mm(kx, qx[...], NT)).astype(BF16)
                        acc[...] += mm(vt[at, ks], p, NN)

    @pl.when(jnp.logical_not(plain))
    def _():
        for _, top, *_ in heads:
            top[...] = jnp.full_like(top, -3e38)

        def per_k(ki, _):
            @pl.when(lax.rem(ki, rows // TILE) < keys[lax.div(ki, rows // TILE)])
            def _():
                ks = tile_at(ki)
                kx = key_side(ks)
                for acc, top, qx, at in heads:
                    s = mm(kx, qx[...], NT)
                    old = top[...]
                    new = jnp.maximum(old, jnp.max(s, axis=0, keepdims=True))
                    p = jnp.exp(s - new[:1, :]).astype(BF16)
                    acc[...] = acc[...] * jnp.exp(old - new)[:1, :] + mm(vt[at, ks], p, NN)
                    top[...] = new
            return 0

        lax.fori_loop(0, near // TILE, per_k, 0)

    def finish(qi, _):
        qs = tile_at(qi)
        tags = qtag_ref[qs, :].astype(F32).T[:8]
        place = lax.broadcasted_iota(jnp.int32, (8, TILE), 0)
        out, ext = [], []
        for acc, top, _, at in heads:
            total, plain_out = (acc[HEAD:, qs], acc[:HEAD, qs]) if at.start == 0 else (acc[:HEAD, qs], acc[HEAD:, qs])
            out.append(plain_out / total)
            hi, mid, lo = (x.astype(F32) for x in parts(jnp.log(total[:8]) + top[:, qs]))
            head = jnp.where(place == 2, hi, jnp.where(place == 3, mid, jnp.where(place == 4, lo, tags)))
            ext += [head, jnp.zeros((HEAD - 8, TILE), F32)]
        o_ref[qs, :] = jnp.concatenate(out, axis=0).T.astype(BF16)
        ext_ref[qs, :] = jnp.concatenate(ext, axis=0).T.astype(BF16)
        return 0

    lax.fori_loop(0, rows // TILE, finish, 0)


def attend(q, k, v, qtag, ktag, keys):
    rows, d = q.shape
    near = k.shape[0]
    part = lambda n: pl.BlockSpec((n, PAIR), lambda p, *_: (0, p))
    fixed = lambda n: pl.BlockSpec((n, PAIR), lambda p, *_: (0, 0))
    return pl.pallas_call(
        attend_kernel,
        grid_spec=pltpu.PrefetchScalarGridSpec(
            num_scalar_prefetch=1,
            grid=(d // PAIR,),
            in_specs=[part(rows), part(near), part(near), fixed(rows), fixed(near)],
            out_specs=[part(rows)] * 2,
            scratch_shapes=[pltpu.VMEM((rows, 2 * PAIR), BF16)] * 2 + [pltpu.VMEM((PAIR + HEAD, near), BF16)]
            + [pltpu.VMEM((PAIR, rows), F32)] * 2 + [pltpu.VMEM((8, rows), F32)] * 2,
        ),
        out_shape=[jax.ShapeDtypeStruct((rows, d), BF16)] * 2,
        compiler_params=pltpu.CompilerParams(vmem_limit_bytes=56 * 2**20),
        cost_estimate=pl.CostEstimate(flops=40 * 10**9, bytes_accessed=16 * 2**20, transcendentals=0),
        name="attend",
    )(keys, q, k, v, qtag, ktag)


def hull(qbits, want, nq):
    first, last = jnp.int32(nq), jnp.int32(0)
    for qi in reversed(range(nq)):
        hit = (qbits[qi] & want) != 0
        last = jnp.where(hit & (last == 0), qi + 1, last)
        first = jnp.where(hit, qi, first)
    return first, jnp.maximum(last - first, 0)


def attend_back_kernel(tk, qbits, kbits, q_ref, k_ref, v_ref, g_ref, o_ref, ext_ref, ktag_ref, near_ref, *refs):
    dq_ref, dk_ref, dv_ref, sums, w_ref, qx0, qx1, gx0, gx1, qt, gt, dq_acc, dk_acc, dv_acc = refs[-14:]
    rows, near = q_ref.shape[0], k_ref.shape[0]
    nq = rows // TILE
    left = left_lanes()
    place = lax.broadcasted_iota(jnp.int32, (1, PAIR), 1) % HEAD
    halves = same_half()

    def per_q(qi, _):
        qs = tile_at(qi)
        q_pair, g_pair, ext = q_ref[qs, :], g_ref[qs, :], ext_ref[qs, :]
        qt[:, qs] = q_pair.T
        gt[:, qs] = g_pair.T
        zero = jnp.zeros_like(q_pair)
        hi, mid, _ = parts(g_pair.astype(F32) * o_ref[qs, :].astype(F32))
        hi, mid, _ = parts(mm(hi, halves, NN) + mm(mid, halves, NN))
        inner = jnp.where(place == 2, hi, jnp.where(place == 3, mid, zero))
        scaled = q_pair * jnp.asarray(SCALE, BF16)
        for x0, x1, base, more in ((qx0, qx1, scaled, ext), (gx0, gx1, g_pair, inner)):
            x0[qs, :PAIR] = jnp.where(left, base, zero)
            x1[qs, :PAIR] = jnp.where(left, zero, base)
            x0[qs, PAIR:] = jnp.where(left, more, zero)
            x1[qs, PAIR:] = jnp.where(left, zero, more)
        return 0

    lax.fori_loop(0, nq, per_q, 0)
    dq_acc[...] = jnp.zeros_like(dq_acc)

    def per_k(ki, _):
        first, count = hull(qbits, kbits[ki], nq)
        ks = tile_at(ki, tk)

        @pl.when(count == 0)
        def _():
            dk_acc[:, ks] = jnp.zeros((PAIR, tk), F32)
            dv_acc[:, ks] = jnp.zeros((PAIR, tk), F32)

        for n in range(1, nq + 1):
            @pl.when(count == n)
            def _():
                qs = pl.ds(pl.multiple_of(first * TILE, TILE), n * TILE)
                k_pair, tags = k_ref[ks, :], ktag_ref[ks, :]
                zero = jnp.zeros_like(k_pair)
                kx = jnp.concatenate([k_pair, tags], axis=1)
                vx = jnp.concatenate([v_ref[ks, :], tags], axis=1)
                dq = 0.0
                for qx, gx, at, kz in ((qx0, gx0, 0, jnp.where(left, k_pair, zero)),
                                       (qx1, gx1, HEAD, jnp.where(left, zero, k_pair))):
                    head = slice(at, at + HEAD)
                    p = jnp.exp(mm(qx[qs, :], kx, NT))
                    ds = (p * mm(gx[qs, :], vx, NT)).astype(BF16)
                    dv_acc[head, ks] = mm(gt[head, qs], p.astype(BF16), NN)
                    dk_acc[head, ks] = mm(qt[head, qs], ds, NN)
                    dq = dq + mm(ds, kz, NN)
                dq_acc[qs, :] += dq
        return 0

    lax.fori_loop(0, near // tk, per_k, 0)
    dq = (dq_acc[...] * SCALE).astype(BF16)
    dk = (dk_acc[...] * SCALE).astype(BF16)
    dv = dv_acc[...].astype(BF16)
    dq_ref[...] = dq
    dk_ref[...] = dk.T
    dv_ref[...] = dv.T
    w_ref[:, :PAIR] = mm(dq, near_ref[:rows, :], TN).T
    w_ref[:, PAIR:2 * PAIR] = mm(dk, near_ref[...], NN).T
    w_ref[:, 2 * PAIR:] = mm(dv, near_ref[...], NN).T
    sums[0:1, :] = col_sum(dq_ref[...].astype(F32))
    sums[1:2, :] = mm(jnp.ones((8, near), BF16), dv_ref[...], NN)[:1]
    sums[2:, :] = jnp.zeros((6, PAIR), F32)


def attend_back(pair, pairs, kept, after, q, k, v, g, o, ext, ktag, near_rows, qbits, kbits, tk):
    rows, d = q.shape
    near = k.shape[0]
    part = lambda n: pl.BlockSpec((n, PAIR), lambda p, *_: (0, pair + p))
    hold = pl.BlockSpec(memory_space=pl.ANY)
    extra = list(kept) + list(after)
    return pl.pallas_call(
        functools.partial(attend_back_kernel, tk),
        grid_spec=pltpu.PrefetchScalarGridSpec(
            num_scalar_prefetch=2,
            grid=(pairs,),
            in_specs=[part(rows), part(near), part(near)] + [part(rows)] * 3 + [pl.BlockSpec((near, PAIR), lambda p, *_: (0, 0)),
               pl.BlockSpec((near, d), lambda p, *_: (0, 0), pipeline_mode=pl.Buffered(1))]
            + [hold] * len(extra),
            out_specs=[part(rows), part(near), part(near), pl.BlockSpec((8, PAIR), lambda p, *_: (0, p)),
                       pl.BlockSpec((d, 3 * PAIR), lambda p, *_: (0, p))],
            scratch_shapes=[pltpu.VMEM((rows, 2 * PAIR), BF16)] * 4 + [pltpu.VMEM((PAIR, rows), BF16)] * 2
            + [pltpu.VMEM((rows, PAIR), F32)] + [pltpu.VMEM((PAIR, near), F32)] * 2,
        ),
        out_shape=[jax.ShapeDtypeStruct((n, d), BF16) for n in (rows, near, near)]
        + [jax.ShapeDtypeStruct((8, pairs * PAIR), F32), jax.ShapeDtypeStruct((d, pairs * 3 * PAIR), F32)],
        input_output_aliases={10 + i: i for i in range(len(kept))},
        compiler_params=pltpu.CompilerParams(vmem_limit_bytes=56 * 2**20),
        cost_estimate=pl.CostEstimate(flops=18 * pairs * 10**9, bytes_accessed=8 * 2**20, transcendentals=0),
        name="attend_back",
    )(qbits, kbits, q, k, v, g, o, ext, ktag, near_rows, *extra)


def row_norm(values):
    centred = values - jnp.mean(values, axis=-1, keepdims=True)
    rstd = lax.rsqrt(jnp.mean(centred * centred, axis=-1, keepdims=True) + 1e-12)
    return centred * rstd, rstd


def norm_back(cot, gain, normed, rstd):
    e = cot * gain
    return rstd * (e - jnp.mean(e, axis=-1, keepdims=True) - normed * jnp.mean(e * normed, axis=-1, keepdims=True))


def dense_kernel(tf, hidden, mixed, out_grad, mask, w_out, w_up, w_down, b_out, gain_one, shift_one, b_up, b_down,
                 gain_two, shift_two, result, low_out, active, d_branch, d_upper, d_one, d_att, d_mixed, sums, sum_up,
                 slope):
    ff = w_up.shape[1]

    @pl.when(pl.program_id(0) == 0)
    def _():
        sums[...] = jnp.zeros_like(sums)
        sum_up[...] = jnp.zeros_like(sum_up)

    vec = lambda ref: ref[...].reshape(1, -1)
    r1 = hidden[...].astype(F32) + (mm(mixed[...], w_out[...], NN) + vec(b_out))
    n1, s1 = row_norm(r1)
    normed_one = n1 * vec(gain_one) + vec(shift_one)
    low = normed_one.astype(BF16)
    low_out[...] = low
    branch = jnp.zeros_like(r1)
    bias = vec(b_up)
    for t in range(0, ff, tf):
        c = pl.ds(t, tf)
        u = mm(low, w_up[:, c], NN) + bias[:, t:t + tf]
        phi = 0.5 + 0.5 * lax.erf(u * (0.5**0.5))
        a = (u * phi).astype(BF16)
        active[:, c] = a
        slope[:, c] = phi + u * (jnp.exp(u * u * -0.5) * 0.3989422804014327)
        branch = branch + mm(a, w_down[c, :], NN)
    n2, s2 = row_norm(normed_one + (branch + vec(b_down)))
    result[...] = (n2 * vec(gain_two) + vec(shift_two)).astype(BF16)
    cot = out_grad[...].astype(F32) * mask[...]
    d_two = norm_back(cot, vec(gain_two), n2, s2)
    db = d_two.astype(BF16)
    d_branch[...] = db
    sums[0:1, :] += col_sum(cot * n2)
    sums[1:2, :] += col_sum(cot)
    sums[2:3, :] += col_sum(db.astype(F32))
    d_normed = d_two
    for t in range(0, ff, tf):
        c = pl.ds(t, tf)
        du = (mm(db, w_down[c, :], NT) * slope[:, c]).astype(BF16)
        d_upper[:, c] = du
        sum_up[:, c] += col_sum(du.astype(F32))
        d_normed = d_normed + mm(du, w_up[:, c], NT)
    sums[3:4, :] += col_sum(d_normed * n1)
    sums[4:5, :] += col_sum(d_normed)
    d1 = norm_back(d_normed, vec(gain_one), n1, s1)
    d_one[...] = d1
    da = d1.astype(BF16)
    d_att[...] = da
    sums[5:6, :] += col_sum(da.astype(F32))
    d_mixed[...] = mm(da, w_out[...], NT).astype(BF16)


def dense(hidden, mixed, out_grad, mask, w_out, w_up, w_down, b_out, gain_one, shift_one, b_up, b_down, gain_two,
          shift_two, tr=256, tf=768):
    rows, d = hidden.shape
    ff = w_up.shape[1]
    row = lambda n: pl.BlockSpec((tr, n), lambda i: (i, 0))
    whole = lambda a, b: pl.BlockSpec((a, b), lambda i: (0, 0), pipeline_mode=pl.Buffered(1))
    flat = lambda n: pl.BlockSpec((n,), lambda i: (0,))
    shape = jax.ShapeDtypeStruct
    low = shape((rows, d), BF16)
    return pl.pallas_call(
        functools.partial(dense_kernel, tf),
        grid=(rows // tr,),
        in_specs=[row(d), row(d), row(d), row(1), whole(d, d), whole(d, ff), whole(ff, d), flat(d), flat(d), flat(d),
                  flat(ff), flat(d), flat(d), flat(d)],
        out_specs=[row(d), row(d), row(ff), row(d), row(ff), row(d), row(d), row(d),
                   pl.BlockSpec((8, d), lambda i: (0, 0)), pl.BlockSpec((1, ff), lambda i: (0, 0))],
        out_shape=[low, low, shape((rows, ff), BF16), low, shape((rows, ff), BF16), shape((rows, d), F32), low, low,
                   shape((8, d), F32), shape((1, ff), F32)],
        scratch_shapes=[pltpu.VMEM((tr, ff), F32)],
        compiler_params=pltpu.CompilerParams(vmem_limit_bytes=56 * 2**20),
        cost_estimate=pl.CostEstimate(flops=40 * 10**9, bytes_accessed=40 * 2**20, transcendentals=0),
        name="dense",
    )(hidden, mixed, out_grad, mask.astype(F32).reshape(-1, 1), w_out, w_up, w_down, b_out, gain_one, shift_one, b_up,
      b_down, gain_two, shift_two)


def back_kernel(dk, dv, w_key, w_value, *refs):
    total = mm(dk[...], w_key[...], NT) + mm(dv[...], w_value[...], NT)
    if len(refs) > 1:
        dq, w_query, kept = refs[:3]
        total = total + mm(dq[...], w_query[...], NT) + kept[...]
    refs[-1][...] = total.astype(refs[-1].dtype)


def back_product(start, rows, dk, dv, w_key, w_value, own=()):
    d = w_key.shape[0]
    tr = 512
    at = lambda i: (start // tr + i, 0)
    row = lambda place: pl.BlockSpec((tr, d), place)
    whole = pl.BlockSpec((d, d), lambda i: (0, 0))
    return pl.pallas_call(
        back_kernel,
        grid=(rows // tr,),
        in_specs=[row(at), row(at), whole, whole] + ([row(lambda i: (i, 0)), whole, row(lambda i: (i, 0))] if own else []),
        out_specs=row(lambda i: (i, 0)),
        out_shape=jax.ShapeDtypeStruct((rows, d), F32 if own else BF16),
        compiler_params=pltpu.CompilerParams(vmem_limit_bytes=40 * 2**20),
        cost_estimate=pl.CostEstimate(flops=(6 if own else 4) * rows * d * d, bytes_accessed=10 * rows * d, transcendentals=0),
        name="back_product",
    )(dk, dv, w_key, w_value, *own)


ALL = ("page", "band")


def everyone():
    return lax.axis_size("page") * lax.axis_size("band")


def swapped(block, mask):
    return lax.ppermute(block, ALL, [(i, i ^ mask) for i in range(everyone())])


def side(bit):
    return lax.rem(lax.div(lax.axis_index(ALL), bit), 2)


def masks_of(bits):
    masks = [0]
    for bit in reversed(bits):
        masks = masks + [mask | bit for mask in masks]
    return masks


def place_of(bits):
    at = 0
    for bit in bits:
        at = 2 * at + side(bit)
    return at


class Summing:
    def __init__(self, block, stages):
        self.stages, self.at = stages, 0
        self.deal(block)

    def deal(self, block):
        masks = masks_of(self.stages[self.at])
        rows = block.shape[0] // len(masks)
        place = place_of(self.stages[self.at])
        part = lambda i: lax.dynamic_slice_in_dim(block, jnp.bitwise_xor(place, i) * rows, rows)
        self.mine = part(0)
        self.others = [part(i).astype(BF16) for i in range(1, len(masks))]

    def advance(self, held=None):
        if self.at < len(self.stages):
            masks = masks_of(self.stages[self.at])
            theirs = [swapped(other, mask) for other, mask in zip(self.others, masks[1:])]
            if held is not None:
                theirs, held = lax.optimization_barrier((theirs, held))
            block = self.mine
            for other in theirs:
                block = block + other.astype(F32)
            self.at += 1
            if self.at < len(self.stages):
                self.deal(block)
            else:
                self.others = [block.astype(BF16)]
        return held

    def finish(self):
        while self.at < len(self.stages):
            self.advance()
        return self.others[0]


def hand_out(block, stages):
    for bits in reversed(stages):
        parts = [block] + [swapped(block, mask) for mask in masks_of(bits)[1:]]
        for i, bit in enumerate(bits):
            far = 1 << (len(bits) - 1 - i)
            flip = side(bit) == 1
            parts = [jnp.where(flip, parts[j ^ far], parts[j]) for j in range(len(parts))]
        block = jnp.concatenate(parts)
    return block


def added_up(vectors, stages):
    for bits in stages:
        parts = [vectors] + [swapped(vectors, mask) for mask in masks_of(bits)[1:]]
        while len(parts) > 1:
            parts = [parts[i] + parts[i + 1] for i in range(0, len(parts), 2)]
        vectors = parts[0]
    return vectors


def gather_all(blocks, orders):
    width = min(block.shape[1] for block in blocks)
    flat = [block[:, c:c + width] for block in blocks for c in range(0, block.shape[1], width)]
    got = lax.all_gather(jnp.concatenate(flat), ALL, axis=0, tiled=False)
    bits = [1 << i for i in reversed(range(everyone().bit_length() - 1))]
    out, at = [], 0
    for block, order in zip(blocks, orders):
        rows = block.shape[0]
        parts = []
        for _ in range(0, block.shape[1], width):
            part = got[:, at:at + rows].reshape([2] * len(bits) + [rows, width])
            part = part.transpose([bits.index(bit) for stage in order for bit in stage] + [len(bits), len(bits) + 1])
            parts.append(part.reshape(-1, width).astype(F32))
            at += rows
        out.append(jnp.concatenate(parts, axis=1))
    return out


def tag_columns(page_ids, near_tags):
    place = jnp.arange(PAIR)[None, :] % HEAD
    qtag = jnp.where(jnp.arange(PAIR)[None, :] == page_ids[:, None], 1.0, 0.0).astype(BF16)
    ktag = jnp.where((place < 2) & (near_tags[:, None] != place + 1), BLOCKED, 0.0)
    return qtag, jnp.where((place >= 2) & (place < 5), -1.0, ktag).astype(BF16)


def tokens_of(near_tags, rows):
    have = jnp.sum((near_tags.reshape(-1, rows) > 0).astype(jnp.int32), axis=1)
    return (have + (TILE - 1)) // TILE


def tile_bits(tags, tile):
    tags = tags.reshape(-1, tile)
    return sum(jnp.max(jnp.where(tags == d + 1, 1 << d, 0), axis=1) for d in range(2)).astype(jnp.int32)


def body(hidden, page_ids, key_mask, out_grad, w_query, b_query, w_key, w_value, b_value, w_out, b_out, gain_one,
         shift_one, w_up, b_up, w_down, b_down, gain_two, shift_two):
    rows, d = hidden.shape
    bands = lax.axis_size("band")
    mates = [(i, i ^ 1) for i in range(bands)]
    across = [(i, i + 1) for i in range(1, bands - 1, 2)] + [(i + 1, i) for i in range(1, bands - 1, 2)]
    to_mate = lambda x: lax.ppermute(x, "band", mates)
    to_across = lambda x: lax.ppermute(x, "band", across)

    key_tags = jnp.where(key_mask == 1, page_ids + 1, 0)
    far = to_across(hidden)
    mate = to_mate(hidden)
    near_tags = jnp.concatenate([key_tags, to_mate(key_tags), to_across(key_tags)])
    queries = (mm(hidden, w_query, NN) + b_query).astype(BF16)
    near = jnp.concatenate([hidden, mate, far])
    keys = mm(near, w_key, NN).astype(BF16)
    values = (mm(near, w_value, NN) + b_value).astype(BF16)
    qtag, ktag = tag_columns(page_ids, near_tags)

    mixed, ext = attend(queries, keys, values, qtag, ktag, tokens_of(near_tags, rows))
    (result, normed_low, active, d_branch, d_upper, d_one, d_att, d_mixed, sums, sum_up) = dense(
        hidden, mixed, out_grad, key_mask, w_out, w_up, w_down, b_out, gain_one, shift_one, b_up, b_down, gain_two,
        shift_two)

    count = everyone().bit_length() - 1
    core, y, x, z = 1, 2, bands, 2 * bands
    rest = [1 << i for i in range(count) if 1 << i not in (core, y, x, z)]
    turns = [[[core]] + [[bit] for bit in order + rest] for order in ([x, y, z], [y, z, x], [z, x, y])]
    direct = [[core], [x, y]] + [([z] + rest)[i:i + 2] for i in range(0, 1 + len(rest), 2)]

    cut = active.shape[1] * 3 // 4
    streams = [Summing(mm(active[:, :cut], d_branch, TN), turns[0])]
    streams.append(Summing(mm(normed_low, d_upper[:, :cut], TN), turns[1]))
    third = [mm(active[:, cut:], d_branch, TN), mm(normed_low, d_upper[:, cut:], TN), mm(mixed, d_att, TN)]
    streams.append(Summing(jnp.concatenate(third, axis=1), turns[2]))
    for stream in streams:
        d_mixed = stream.advance(d_mixed)
    after = [other for stream in streams for other in stream.others]

    tk = 512
    bits = (tile_bits(key_tags, TILE), tile_bits(near_tags, tk))
    pairs = d // PAIR
    kept, end_sums, groups, at, parts = (), [], [], 0, []
    for size in [1] * (pairs - 2) + [2]:
        *kept, part_sums, part = attend_back(at, size, kept, after, queries, keys, values, d_mixed, mixed, ext, ktag, near,
                                             *bits, tk)
        at += size
        end_sums.append(part_sums)
        parts.append(part)
        if at < pairs:
            after = []
            for stream in streams:
                kept[0] = stream.advance(kept[0])
                after = after + stream.others
        if at % 2 == 0:
            group = Summing(jnp.concatenate(parts, axis=1), direct)
            parts = []
            groups.append(group)
            streams = streams + [group]
            after = after + group.others
    dq, dk, dv = kept

    first, second, third = gather_all([stream.finish() for stream in streams[:3]], turns)
    grad_down = jnp.concatenate([first, third[:, :d]])
    grad_up = jnp.concatenate([second, third[:, d:2 * d]], axis=1)
    grad_out = third[:, 2 * d:]

    vectors = [sums, sum_up.reshape(-1, d)] + [jnp.concatenate([e[i:i + 1] for e in end_sums], axis=1) for i in (0, 1)]
    vectors = added_up(jnp.concatenate(vectors), direct)

    far_part = to_across(back_product(2 * rows, rows, dk, dv, w_key, w_value))
    mate_part = to_mate(back_product(rows, rows, dk, dv, w_key, w_value))
    own_part = back_product(0, rows, dk, dv, w_key, w_value, (dq, w_query, d_one))
    input_grad = (own_part + mate_part.astype(F32) + far_part.astype(F32)).astype(BF16)

    groups = [hand_out(group.finish(), direct).astype(F32).reshape(d, 2, 3, PAIR) for group in groups]
    grads = [jnp.concatenate([group[:, p, i] for group in groups for p in range(2)], axis=1) for i in range(3)]
    ups = 8 + sum_up.size // d
    return (
        result,
        input_grad,
        grads[0],
        vectors[ups],
        grads[1],
        grads[2],
        vectors[ups + 1],
        grad_out,
        vectors[5],
        vectors[3],
        vectors[4],
        grad_up,
        vectors[8:ups].reshape(-1),
        grad_down,
        vectors[2],
        vectors[0],
        vectors[1],
    )


def solution(mesh):
    split = P(("page", "band"), None)
    line = P(("page", "band"))
    return jax.shard_map(
        body,
        mesh=mesh,
        in_specs=(split, line, line, split) + (P(),) * 15,
        out_specs=(split, split) + (P(),) * 15,
        check_vma=False,
    )
```

time: 1880 us -> 597 us (0.32); the launches traced: 1850 us -> 594 us
  matrix products: 593 us -> 34.1 us
  local copies, waits for them, and re-layouts: 507 us -> 80.4 us
  blocking collectives: 303 us -> 0 us
  other arithmetic: 286 us -> 55.2 us
  Pallas kernels: 0 us -> 200 us
  starting transfers between devices: 45.3 us -> 175 us
  waiting for transfers between devices: 102 us -> 33 us
    dot_general x60 -> x8, matrix products: 593 us -> 34.1 us  [mm(): return lax.dot_general(a, b, dims, preferred_element_type=F32)]
    unnamed x1 -> x0, blocking collectives: 303 us -> none
    unnamed x134 -> x151, local copies, waits for them, and re-layouts: 255 us -> 38.1 us
    pallas_call x0 -> x10, Pallas kernels: none -> 200 us  [the longest x5 98.1 us: attend_back(): pl.pallas_call(functools.partial(attend_back_kernel, tk), grid_spec=pltpu...]
    ppermute x6 -> x70, starting transfers between devices: 41.1 us -> 175 us  [the longest x64 168 us: swapped(): return lax.ppermute(block, ALL, [(i, i ^ mask) for i in range(everyone())])]
    convert_element_type x8 -> x12, other arithmetic: 113 us -> 11 us  [the longest x3 4.34 us: body(): hand_out(group.finish(), direct).astype(F32).reshape(d, 2, 3, PAIR)]
    all_gather x1, waiting for transfers between devices: 101 us -> 0.01 us  [gather_all(): got = lax.all_gather(jnp.concatenate(flat), ALL, axis=0, tiled=False)]
    reduce_sum x14 -> x1, other arithmetic: 82.9 us -> 0.13 us  [tokens_of(): have = jnp.sum((near_tags.reshape(-1, rows) > 0).astype(jnp.int32), axis=1)]
  transfers between devices with their start and end apart: 8 -> 71, of which waited for: 2 -> 27; matrix products, arithmetic and copies ran while one was open for 3% -> 16% of each run, Pallas kernels for 0% -> 19%
where the time goes in v1:
time: 597 us; the launch traced here: 594 us
  Pallas kernels  200 us (34%)
  starting transfers between devices  175 us (29%)
  local copies, waits for them, and re-layouts  80.4 us (13%)
  other arithmetic  55.2 us (9%)
  matrix products  34.1 us (6%)
  waiting for transfers between devices  33 us (6%)
  between operations  15.7 us (3%)
    ppermute x64, starting transfers between devices, swapped(): return lax.ppermute(block, ALL, [(i, i ^ mask) for i in range(everyone())])  168 us
    pallas_call x5, Pallas kernels, attend_back(): pl.pallas_call(functools.partial(attend_back_kernel, tk), grid_spec=pltpu...  98.1 us
    pallas_call x1, Pallas kernels, attend(): pl.pallas_call(attend_kernel, grid_spec=pltpu.PrefetchScalarGridSpec(num_...  51.6 us
    unnamed x151, local copies, waits for them, and re-layouts  38.1 us
    pallas_call x1, Pallas kernels, dense(): pl.pallas_call(functools.partial(dense_kernel, tf), grid=(rows // tr,), i...  37.5 us
    dot_general x8, matrix products, mm(): return lax.dot_general(a, b, dims, preferred_element_type=F32)  34.1 us
    ppermute x64, waiting for transfers between devices, swapped(): return lax.ppermute(block, ALL, [(i, i ^ mask) for i in range(everyone())])  33 us
    add x18, other arithmetic, advance(): block = block + other.astype(F32)  18.9 us
  transfers between devices with their start and end apart: 71, of which 27 were waited for; matrix products, arithmetic and copies ran while one was open for 16% of the time, Pallas kernels for 19%

profile of v1, /device:TPU:0, one launch (start us, length us, event | category | flops | bytes accessed | tf_op | source)
XLA Modules:
  0.0 594.4 jit_solution(14712570003556629247)
XLA Ops:
  8.8 4.4 collective-permute-start
  14.0 4.3 add_convert_fusion.2.q_ref
  22.3 2.1 select_convert_fusion.ktag_ref
  24.4 2.7 constant_dynamic-update-slice_fusion.1
  28.9 8.1 %convolution_convert_fusion.k_ref = bf16[3072,768]{1,0:T(8,128)(2,1)} fusion(bf16[3072,768]{1,0:T(8,128)(2,1)} %constant_dynamic-update-slice_fusion.near_ref, bf16[768,768]{1,0:T(8,128)(2,1)S(1)} %copy-done.2), kind=kOutput, calls=%fused_computation.2 | convolution fusion | flops 3626237952 | bytes 10616832 | tf_op jit(solution)/shard_map/dot_general | solution.py:25
  37.0 5.5 add_convert_fusion.v_ref
  42.5 51.6 %attend.1 = (bf16[1024,768]{1,0:T(8,128)(2,1)}, bf16[1024,768]{1,0:T(8,128)(2,1)}) custom-call(s32[3]{0:T(128)} %and_select_fusion.1.keys, bf16[1024,768]{1,0:T(8,128)(2,1)} %add_convert_fusion.2.q_ref, bf16[3072,768]{1,0:T(8,128)(2,1)} %convolution_convert_fusion.k_ref, bf16[3072,768]{1,0:T(8,128)(2,1)} %add_convert_fusion.v_ref, ...), custom_call_target="tpu_custom_call" | custom-call | flops 40000000000 | bytes 16777216 | tf_op jit(solution)/shard_map/attend/pallas_call | solution.py:135
  94.2 37.5 %dense.1 = (bf16[1024,768]{1,0:T(8,128)(2,1)}, bf16[1024,768]{1,0:T(8,128)(2,1)}, bf16[1024,3072]{1,0:T(8,128)(2,1)}, bf16[1024,768]{1,0:T(8,128)(2,1)}, bf16[10...) custom-call(bf16[1024,768]{1,0:T(8,128)(2,1)} %hidden.1, ...), custom_call_target="tpu_custom_call" | custom-call | flops 40000000000 | bytes 41943040 | tf_op jit(solution)/shard_map/dense/pallas_call | solution.py:333
  131.7 3.5 fusion.4
  135.4 5.5 fusion.2
  142.5 3.9 fusion
  148.5 59.0 %collective-permute-start.5 = (bf16[384,2304]{1,0:T(8,128)(2,1)S(1)}, bf16[384,2304]{1,0:T(8,128)(2,1)}, u32[]{:S(2)}, u32[]{:S(2)}) collective-permute-start(bf16[384,2304]{1,0:T(8,128)(2,1)S(1)} %dynamic-slice_convert_fusion.1), channel_id=1, source_target_pairs={{0,1},{1,0},{2,3},{3,2},{4,5},{5,4},{6,7},{7,6},{8,9},{9,8},{10,11... | collective-permute-start | bytes 5308424 | tf_op jit(solution)/shard_map/ppermute | solution.py:384
  209.1 2.8 copy-done.9
  218.7 3.0 convert_add_fusion.1
  223.2 2.0 convert_add_fusion
  230.7 9.8 %collective-permute-start.9 = (bf16[576,768]{1,0:T(8,128)(2,1)}, bf16[576,768]{1,0:T(8,128)(2,1)}, u32[]{:S(2)}, u32[]{:S(2)}) collective-permute-start(bf16[576,768]{1,0:T(8,128)(2,1)} %dynamic-slice_convert_fusion.5.refs_0_), channel_id=1, source_target_pairs={{0,4},{1,5},{2,6},{3,7},{4,0},{5,1},{6,2},{7,3},{8,12},{9,13},{10,... | collective-permute-start | bytes 2654216 | tf_op jit(solution)/shard_map/ppermute | solution.py:384
  240.5 17.1 %attend_back.5 = (bf16[1024,768]{1,0:T(8,128)(2,1)}, bf16[3072,768]{1,0:T(8,128)(2,1)}, bf16[3072,768]{1,0:T(8,128)(2,1)}, f32[8,128]{1,0:T(8,128)}, f32[768,384]{1,0:T(8,128)}) custom-call(s32[4]{0:T(128)} %add.390.qbits, s32[6]{0:T(128)} %add.391.kbits, bf16[1024,768]{1,0:T(8,128)(2,1)} %add_convert_fusion.2.q_ref, ...), custom_call_target="tpu_custom_call" | custom-call | flops 17999998976 | bytes 8388608 | tf_op jit(solution)/shard_map/attend_back/pallas_call | solution.py:239
  257.6 2.4 constant_dynamic-update-slice_fusion.4
  260.5 1.9 convert_add_fusion.3
  269.2 4.3 collective-permute-start.13
  273.5 17.1 %attend_back.6 = (bf16[1024,768]{1,0:T(8,128)(2,1)}, bf16[3072,768]{1,0:T(8,128)(2,1)}, bf16[3072,768]{1,0:T(8,128)(2,1)}, f32[8,128]{1,0:T(8,128)}, f32[768,384]{1,0:T(8,128)}) custom-call(s32[4]{0:T(128)} %add.390.qbits, s32[6]{0:T(128)} %add.391.kbits, ...), custom_call_target="tpu_custom_call", output_to_operand_aliasing={{0}: (10, {}), {1}: (11, {}), {2}: (12, {})} | custom-call | flops 17999998976 | bytes 8388608 | tf_op jit(solution)/shard_map/attend_back/pallas_call | solution.py:239
  294.1 5.4 collective-permute-start.14
  301.3 2.5 collective-permute-start.15
  305.7 17.1 %attend_back.7 = (bf16[1024,768]{1,0:T(8,128)(2,1)}, bf16[3072,768]{1,0:T(8,128)(2,1)}, bf16[3072,768]{1,0:T(8,128)(2,1)}, f32[8,128]{1,0:T(8,128)}, f32[768,384]{1,0:T(8,128)}) custom-call(s32[4]{0:T(128)} %add.390.qbits, s32[6]{0:T(128)} %add.391.kbits, ...), custom_call_target="tpu_custom_call", output_to_operand_aliasing={{0}: (10, {}), {1}: (11, {}), {2}: (12, {})} | custom-call | flops 17999998976 | bytes 8388608 | tf_op jit(solution)/shard_map/attend_back/pallas_call | solution.py:239
  331.6 17.2 %attend_back.8 = (bf16[1024,768]{1,0:T(8,128)(2,1)}, bf16[3072,768]{1,0:T(8,128)(2,1)}, bf16[3072,768]{1,0:T(8,128)(2,1)}, f32[8,128]{1,0:T(8,128)}, f32[768,384]{1,0:T(8,128)}) custom-call(s32[4]{0:T(128)} %add.390.qbits, s32[6]{0:T(128)} %add.391.kbits, ...), custom_call_target="tpu_custom_call", output_to_operand_aliasing={{0}: (10, {}), {1}: (11, {}), {2}: (12, {})} | custom-call | flops 17999998976 | bytes 8388608 | tf_op jit(solution)/shard_map/attend_back/pallas_call | solution.py:239
  354.3 9.0 %collective-permute-start.17 = (bf16[96,768]{1,0:T(8,128)(2,1)S(1)}, bf16[96,768]{1,0:T(8,128)(2,1)S(1)}, u32[]{:S(2)}, u32[]{:S(2)}) collective-permute-start(bf16[96,768]{1,0:T(8,128)(2,1)S(1)} %copy-done.46), channel_id=1, source_target_pairs={{0,2},{1,3},{2,0},{3,1},{4,6},{5,7},{6,4},{7,5},{8,10},{9,11},{10,... | collective-permute-start | bytes 442376 | tf_op jit(solution)/shard_map/ppermute | solution.py:384
  366.8 2.7 collective-permute-done.18
  371.3 3.4 collective-permute-start.27
  377.0 29.6 %attend_back.9 = (bf16[1024,768]{1,0:T(8,128)(2,1)}, bf16[3072,768]{1,0:T(8,128)(2,1)}, bf16[3072,768]{1,0:T(8,128)(2,1)}, f32[8,256]{1,0:T(8,128)}, f32[768,768]{1,0:T(8,128)}) custom-call(s32[4]{0:T(128)} %add.390.qbits, s32[6]{0:T(128)} %add.391.kbits, ...), custom_call_target="tpu_custom_call", output_to_operand_aliasing={{0}: (10, {}), {1}: (11, {}), {2}: (12, {})} | custom-call | flops 35999997952 | bytes 8388608 | tf_op jit(solution)/shard_map/attend_back/pallas_call | solution.py:239
  406.6 2.3 copy-done
  409.0 2.3 copy-done.1
  411.3 3.7 back_product.5
  416.9 2.1 dynamic-slice_convert_fusion.6
  419.8 4.0 back_product.4
  423.9 5.5 back_product.3
  429.4 10.8 %collective-permute-start.63 = (f32[14,768]{1,0:T(8,128)S(1)}, f32[14,768]{1,0:T(8,128)S(1)}, u32[]{:S(2)}, u32[]{:S(2)}) collective-permute-start(f32[14,768]{1,0:T(8,128)S(1)} %pad_maximum_fusion.7), channel_id=1, source_target_pairs={{0,1},{1,0},{2,3},{3,2},{4,5},{5,4},{6,7},{7,6},{8,9},{9,8},{10,11... | collective-permute-start | bytes 129032 | tf_op jit(solution)/shard_map/ppermute | solution.py:384
  440.3 3.4 collective-permute-start.29
  444.7 2.4 collective-permute-done.28
  447.1 3.6 collective-permute-start.65
  450.7 3.7 collective-permute-start.66
  456.5 2.0 collective-permute-done.64
  458.6 2.0 collective-permute-start.69
  468.7 2.4 collective-permute-done.31
  482.8 1.9 collective-permute-start.41
  485.1 2.1 collective-permute-start.39
  499.3 2.6 collective-permute-done.52
  505.2 2.7 collective-permute-start.53
  510.1 2.2 collective-permute-start.56
  515.8 2.1 copy.89
  517.9 2.1 copy.88
  525.8 2.5 collective-permute-done.46
  539.5 2.1 copy.91
  541.6 2.1 copy.90
  547.3 2.3 broadcast_select_fusion.1
  549.6 2.1 copy.93
  551.7 2.1 copy.92
  557.3 3.0 copy.101
  560.4 3.0 copy.102
  563.4 3.3 copy.103
  566.7 3.5 add_convert_fusion.1
  570.2 3.5 fusion.27
  573.7 2.2 slice.251
  578.4 4.5 maximum_convert_fusion.1
  582.9 4.3 maximum_convert_fusion
  (376 shorter events, 136.5 us)
Async XLA Ops:
  7.2 563.0 %all-gather.3.cloned.1.call-start = ((), (), s32[]{:S(2)}) async-start(), calls=%async_computation | async-start | bytes 10948608 | tf_op jit(solution)/shard_map/all_gather | solution.py:463
  8.0 13.6 %collective-permute-start.1 = (s32[1024]{0:T(1024)S(1)}, s32[1024]{0:T(1024)S(1)}, u32[]{:S(2)}, u32[]{:S(2)}) collective-permute-start(s32[1024]{0:T(1024)S(1)} %get-tuple-element.210), channel_id=1, source_target_pairs={{1,2},{2,1},{5,6},{6,5},{9,10},{10,9},{13,14},{14,13},{17,18},{18,... | collective-permute-start | bytes 12296 | tf_op jit(solution)/shard_map/ppermute | solution.py:502
  8.8 12.8 %collective-permute-start = (s32[1024]{0:T(1024)S(1)}, s32[1024]{0:T(1024)S(1)}, u32[]{:S(2)}, u32[]{:S(2)}) collective-permute-start(s32[1024]{0:T(1024)S(1)} %get-tuple-element.210), channel_id=1, source_target_pairs={{0,1},{1,0},{2,3},{3,2},{4,5},{5,4},{6,7},{7,6},{8,9},{9,8},{10,11... | collective-permute-start | bytes 12296 | tf_op jit(solution)/shard_map/ppermute | solution.py:501
  13.2 11.2 %collective-permute-start.2 = (bf16[1024,768]{1,0:T(8,128)(2,1)}, bf16[1024,768]{1,0:T(8,128)(2,1)}, u32[]{:S(2)}, u32[]{:S(2)}) collective-permute-start(bf16[1024,768]{1,0:T(8,128)(2,1)} %hidden.1), channel_id=1, source_target_pairs={{0,1},{1,0},{2,3},{3,2},{4,5},{5,4},{6,7},{7,6},{8,9},{9,8},{10,11... | collective-permute-start | bytes 4718600 | tf_op jit(solution)/shard_map/ppermute | solution.py:501
  13.3 13.8 %collective-permute-start.3 = (bf16[1024,768]{1,0:T(8,128)(2,1)}, bf16[1024,768]{1,0:T(8,128)(2,1)S(1)}, u32[]{:S(2)}, u32[]{:S(2)}) collective-permute-start(bf16[1024,768]{1,0:T(8,128)(2,1)} %hidden.1), channel_id=1, source_target_pairs={{1,2},{2,1},{5,6},{6,5},{9,10},{10,9},{13,14},{14,13},{17,18},{18,... | collective-permute-start | bytes 4718600 | tf_op jit(solution)/shard_map/ppermute | solution.py:502
  148.5 70.1 %collective-permute-start.5 = (bf16[384,2304]{1,0:T(8,128)(2,1)S(1)}, bf16[384,2304]{1,0:T(8,128)(2,1)}, u32[]{:S(2)}, u32[]{:S(2)}) collective-permute-start(bf16[384,2304]{1,0:T(8,128)(2,1)S(1)} %dynamic-slice_convert_fusion.1), channel_id=1, source_target_pairs={{0,1},{1,0},{2,3},{3,2},{4,5},{5,4},{6,7},{7,6},{8,9},{9,8},{10,11... | collective-permute-start | bytes 5308424 | tf_op jit(solution)/shard_map/ppermute | solution.py:384
  207.7 10.9 %collective-permute-start.6 = (bf16[1152,768]{1,0:T(8,128)(2,1)S(1)}, bf16[1152,768]{1,0:T(8,128)(2,1)}, u32[]{:S(2)}, u32[]{:S(2)}) collective-permute-start(bf16[1152,768]{1,0:T(8,128)(2,1)S(1)} %dynamic-slice_convert_fusion), channel_id=1, source_target_pairs={{0,1},{1,0},{2,3},{3,2},{4,5},{5,4},{6,7},{7,6},{8,9},{9,8},{10,11... | collective-permute-start | bytes 5308424 | tf_op jit(solution)/shard_map/ppermute | solution.py:384
  213.3 5.4 collective-permute-start.4
  226.3 34.2 %collective-permute-start.7 = (bf16[192,2304]{1,0:T(8,128)(2,1)}, bf16[192,2304]{1,0:T(8,128)(2,1)}, u32[]{:S(2)}, u32[]{:S(2)}) collective-permute-start(bf16[192,2304]{1,0:T(8,128)(2,1)} %dynamic-slice_convert_fusion.3.refs_2_), channel_id=1, source_target_pairs={{0,8},{1,9},{2,10},{3,11},{4,12},{5,13},{6,14},{7,15},{8,0},{9,1},... | collective-permute-start | bytes 2654216 | tf_op jit(solution)/shard_map/ppermute | solution.py:384
  227.5 33.0 %collective-permute-start.8 = (bf16[192,2304]{1,0:T(8,128)(2,1)}, bf16[192,2304]{1,0:T(8,128)(2,1)}, u32[]{:S(2)}, u32[]{:S(2)}) collective-permute-start(bf16[192,2304]{1,0:T(8,128)(2,1)} %dynamic-slice_convert_fusion.4.refs_1_), channel_id=1, source_target_pairs={{0,2},{1,3},{2,0},{3,1},{4,6},{5,7},{6,4},{7,5},{8,10},{9,11},{10,... | collective-permute-start | bytes 2654216 | tf_op jit(solution)/shard_map/ppermute | solution.py:384
  230.7 29.8 %collective-permute-start.9 = (bf16[576,768]{1,0:T(8,128)(2,1)}, bf16[576,768]{1,0:T(8,128)(2,1)}, u32[]{:S(2)}, u32[]{:S(2)}) collective-permute-start(bf16[576,768]{1,0:T(8,128)(2,1)} %dynamic-slice_convert_fusion.5.refs_0_), channel_id=1, source_target_pairs={{0,4},{1,5},{2,6},{3,7},{4,0},{5,1},{6,2},{7,3},{8,12},{9,13},{10,... | collective-permute-start | bytes 2654216 | tf_op jit(solution)/shard_map/ppermute | solution.py:384
  263.4 29.3 %collective-permute-start.11 = (bf16[96,2304]{1,0:T(8,128)(2,1)}, bf16[96,2304]{1,0:T(8,128)(2,1)}, u32[]{:S(2)}, u32[]{:S(2)}) collective-permute-start(bf16[96,2304]{1,0:T(8,128)(2,1)} %dynamic-slice_convert_fusion.9.refs_5_), channel_id=1, source_target_pairs={{0,4},{1,5},{2,6},{3,7},{4,0},{5,1},{6,2},{7,3},{8,12},{9,13},{10,... | collective-permute-start | bytes 1327112 | tf_op jit(solution)/shard_map/ppermute | solution.py:384
  267.3 25.3 %collective-permute-start.12 = (bf16[96,2304]{1,0:T(8,128)(2,1)}, bf16[96,2304]{1,0:T(8,128)(2,1)}, u32[]{:S(2)}, u32[]{:S(2)}) collective-permute-start(bf16[96,2304]{1,0:T(8,128)(2,1)} %dynamic-slice_convert_fusion.10.refs_4_), channel_id=1, source_target_pairs={{0,8},{1,9},{2,10},{3,11},{4,12},{5,13},{6,14},{7,15},{8,0},{9,1},... | collective-permute-start | bytes 1327112 | tf_op jit(solution)/shard_map/ppermute | solution.py:384
  269.2 23.4 %collective-permute-start.13 = (bf16[288,768]{1,0:T(8,128)(2,1)S(1)}, bf16[288,768]{1,0:T(8,128)(2,1)S(1)}, u32[]{:S(2)}, u32[]{:S(2)}) collective-permute-start(bf16[288,768]{1,0:T(8,128)(2,1)S(1)} %dynamic-slice_convert_fusion.11.refs_3_), channel_id=1, source_target_pairs={{0,2},{1,3},{2,0},{3,1},{4,6},{5,7},{6,4},{7,5},{8,10},{9,11},{10,... | collective-permute-start | bytes 1327112 | tf_op jit(solution)/shard_map/ppermute | solution.py:384
  292.2 31.4 %collective-permute-start.10 = (bf16[384,768]{1,0:T(8,128)(2,1)S(1)}, bf16[384,768]{1,0:T(8,128)(2,1)S(1)}, u32[]{:S(2)}, u32[]{:S(2)}) collective-permute-start(bf16[384,768]{1,0:T(8,128)(2,1)S(1)} %dynamic-slice_convert_fusion.8.refs_6_), channel_id=1, source_target_pairs={{0,1},{1,0},{2,3},{3,2},{4,5},{5,4},{6,7},{7,6},{8,9},{9,8},{10,11... | collective-permute-start | bytes 1769480 | tf_op jit(solution)/shard_map/ppermute | solution.py:384
  294.1 29.5 %collective-permute-start.14 = (bf16[48,2304]{1,0:T(8,128)(2,1)S(1)}, bf16[48,2304]{1,0:T(8,128)(2,1)}, u32[]{:S(2)}, u32[]{:S(2)}) collective-permute-start(bf16[48,2304]{1,0:T(8,128)(2,1)S(1)} %dynamic-slice_convert_fusion.14.refs_5_), channel_id=1, source_target_pairs={{0,2},{1,3},{2,0},{3,1},{4,6},{5,7},{6,4},{7,5},{8,10},{9,11},{10,... | collective-permute-start | bytes 663560 | tf_op jit(solution)/shard_map/ppermute | solution.py:384
  301.3 22.2 %collective-permute-start.15 = (bf16[48,2304]{1,0:T(8,128)(2,1)}, bf16[48,2304]{1,0:T(8,128)(2,1)}, u32[]{:S(2)}, u32[]{:S(2)}) collective-permute-start(bf16[48,2304]{1,0:T(8,128)(2,1)} %dynamic-slice_convert_fusion.13.refs_4_), channel_id=1, source_target_pairs={{0,4},{1,5},{2,6},{3,7},{4,0},{5,1},{6,2},{7,3},{8,12},{9,13},{10,... | collective-permute-start | bytes 663560 | tf_op jit(solution)/shard_map/ppermute | solution.py:384
  305.0 17.9 %collective-permute-start.16 = (bf16[144,768]{1,0:T(8,128)(2,1)S(1)}, bf16[144,768]{1,0:T(8,128)(2,1)S(1)}, u32[]{:S(2)}, u32[]{:S(2)}) collective-permute-start(bf16[144,768]{1,0:T(8,128)(2,1)S(1)} %dynamic-slice_convert_fusion.12.refs_3_), channel_id=1, source_target_pairs={{0,8},{1,9},{2,10},{3,11},{4,12},{5,13},{6,14},{7,15},{8,0},{9,1},... | collective-permute-start | bytes 663560 | tf_op jit(solution)/shard_map/ppermute | solution.py:384
  324.8 24.1 %collective-permute-start.20 = (bf16[24,2304]{1,0:T(8,128)(2,1)S(1)}, bf16[24,2304]{1,0:T(8,128)(2,1)S(1)}, u32[]{:S(2)}, u32[]{:S(2)}) collective-permute-start(bf16[24,2304]{1,0:T(8,128)(2,1)S(1)} %dynamic-slice_convert_fusion.26.refs_5_), channel_id=1, source_target_pairs={{0,16},{1,17},{2,18},{3,19},{4,20},{5,21},{6,22},{7,23},{8,24},{9,... | collective-permute-start | bytes 331784 | tf_op jit(solution)/shard_map/ppermute | solution.py:384
  327.7 21.2 %collective-permute-start.21 = (bf16[24,2304]{1,0:T(8,128)(2,1)S(1)}, bf16[24,2304]{1,0:T(8,128)(2,1)S(1)}, u32[]{:S(2)}, u32[]{:S(2)}) collective-permute-start(bf16[24,2304]{1,0:T(8,128)(2,1)S(1)} %dynamic-slice_convert_fusion.25.refs_4_), channel_id=1, source_target_pairs={{0,16},{1,17},{2,18},{3,19},{4,20},{5,21},{6,22},{7,23},{8,24},{9,... | collective-permute-start | bytes 331784 | tf_op jit(solution)/shard_map/ppermute | solution.py:384
  328.9 20.0 %collective-permute-start.22 = (bf16[72,768]{1,0:T(8,128)(2,1)S(1)}, bf16[72,768]{1,0:T(8,128)(2,1)S(1)}, u32[]{:S(2)}, u32[]{:S(2)}) collective-permute-start(bf16[72,768]{1,0:T(8,128)(2,1)S(1)} %dynamic-slice_convert_fusion.24.refs_3_), channel_id=1, source_target_pairs={{0,16},{1,17},{2,18},{3,19},{4,20},{5,21},{6,22},{7,23},{8,24},{9,... | collective-permute-start | bytes 331784 | tf_op jit(solution)/shard_map/ppermute | solution.py:384
  354.3 12.5 %collective-permute-start.17 = (bf16[96,768]{1,0:T(8,128)(2,1)S(1)}, bf16[96,768]{1,0:T(8,128)(2,1)S(1)}, u32[]{:S(2)}, u32[]{:S(2)}) collective-permute-start(bf16[96,768]{1,0:T(8,128)(2,1)S(1)} %copy-done.46), channel_id=1, source_target_pairs={{0,2},{1,3},{2,0},{3,1},{4,6},{5,7},{6,4},{7,5},{8,10},{9,11},{10,... | collective-permute-start | bytes 442376 | tf_op jit(solution)/shard_map/ppermute | solution.py:384
  363.3 6.2 %collective-permute-start.18 = (bf16[96,768]{1,0:T(8,128)(2,1)S(1)}, bf16[96,768]{1,0:T(8,128)(2,1)S(1)}, u32[]{:S(2)}, u32[]{:S(2)}) collective-permute-start(bf16[96,768]{1,0:T(8,128)(2,1)S(1)} %copy-done.45), channel_id=1, source_target_pairs={{0,4},{1,5},{2,6},{3,7},{4,0},{5,1},{6,2},{7,3},{8,12},{9,13},{10,... | collective-permute-start | bytes 442376 | tf_op jit(solution)/shard_map/ppermute | solution.py:384
  363.9 7.3 %collective-permute-start.19 = (bf16[96,768]{1,0:T(8,128)(2,1)S(1)}, bf16[96,768]{1,0:T(8,128)(2,1)S(1)}, u32[]{:S(2)}, u32[]{:S(2)}) collective-permute-start(bf16[96,768]{1,0:T(8,128)(2,1)S(1)} %copy-done.44), channel_id=1, source_target_pairs={{0,6},{1,7},{2,4},{3,5},{4,2},{5,3},{6,0},{7,1},{8,14},{9,15},{10,... | collective-permute-start | bytes 442376 | tf_op jit(solution)/shard_map/ppermute | solution.py:384
  365.9 107.1 %collective-permute-start.35 = (bf16[384,768]{1,0:T(8,128)(2,1)}, bf16[384,768]{1,0:T(8,128)(2,1)}, u32[]{:S(2)}, u32[]{:S(2)}) collective-permute-start(bf16[384,768]{1,0:T(8,128)(2,1)} %dynamic-slice_convert_fusion.7.refs_9_), channel_id=1, source_target_pairs={{0,1},{1,0},{2,3},{3,2},{4,5},{5,4},{6,7},{7,6},{8,9},{9,8},{10,11... | collective-permute-start | bytes 1769480 | tf_op jit(solution)/shard_map/ppermute | solution.py:384
  371.3 58.1 %collective-permute-start.27 = (bf16[24,768]{1,0:T(8,128)(2,1)S(1)}, bf16[24,768]{1,0:T(8,128)(2,1)S(1)}, u32[]{:S(2)}, u32[]{:S(2)}) collective-permute-start(bf16[24,768]{1,0:T(8,128)(2,1)S(1)} %get-tuple-element.265.refs_8_), channel_id=1, source_target_pairs={{0,24},{1,25},{2,26},{3,27},{4,28},{5,29},{6,30},{7,31},{8,16},{9,... | collective-permute-start | bytes 110600 | tf_op jit(solution)/shard_map/ppermute | solution.py:384
  374.7 65.5 %collective-permute-start.26 = (bf16[24,768]{1,0:T(8,128)(2,1)S(1)}, bf16[24,768]{1,0:T(8,128)(2,1)S(1)}, u32[]{:S(2)}, u32[]{:S(2)}) collective-permute-start(bf16[24,768]{1,0:T(8,128)(2,1)S(1)} %get-tuple-element.266.refs_7_), channel_id=1, source_target_pairs={{0,8},{1,9},{2,10},{3,11},{4,12},{5,13},{6,14},{7,15},{8,0},{9,1},... | collective-permute-start | bytes 110600 | tf_op jit(solution)/shard_map/ppermute | solution.py:384
  375.6 64.6 %collective-permute-start.25 = (bf16[24,768]{1,0:T(8,128)(2,1)S(1)}, bf16[24,768]{1,0:T(8,128)(2,1)S(1)}, u32[]{:S(2)}, u32[]{:S(2)}) collective-permute-start(bf16[24,768]{1,0:T(8,128)(2,1)S(1)} %get-tuple-element.267.refs_6_), channel_id=1, source_target_pairs={{0,16},{1,17},{2,18},{3,19},{4,20},{5,21},{6,22},{7,23},{8,24},{9,... | collective-permute-start | bytes 110600 | tf_op jit(solution)/shard_map/ppermute | solution.py:384
  415.0 151.7 %collective-permute-start.24 = (bf16[1024,768]{1,0:T(8,128)(2,1)}, bf16[1024,768]{1,0:T(8,128)(2,1)}, u32[]{:S(2)}, u32[]{:S(2)}) collective-permute-start(bf16[1024,768]{1,0:T(8,128)(2,1)} %back_product.5), channel_id=1, source_target_pairs={{1,2},{2,1},{5,6},{6,5},{9,10},{10,9},{13,14},{14,13},{17,18},{18,... | collective-permute-start | bytes 4718600 | tf_op jit(solution)/shard_map/ppermute | solution.py:502
  429.4 14.3 %collective-permute-start.63 = (f32[14,768]{1,0:T(8,128)S(1)}, f32[14,768]{1,0:T(8,128)S(1)}, u32[]{:S(2)}, u32[]{:S(2)}) collective-permute-start(f32[14,768]{1,0:T(8,128)S(1)} %pad_maximum_fusion.7), channel_id=1, source_target_pairs={{0,1},{1,0},{2,3},{3,2},{4,5},{5,4},{6,7},{7,6},{8,9},{9,8},{10,11... | collective-permute-start | bytes 129032 | tf_op jit(solution)/shard_map/ppermute | solution.py:384
  440.2 6.9 %collective-permute-start.28 = (bf16[24,768]{1,0:T(8,128)(2,1)S(1)}, bf16[24,768]{1,0:T(8,128)(2,1)S(1)}, u32[]{:S(2)}, u32[]{:S(2)}) collective-permute-start(bf16[24,768]{1,0:T(8,128)(2,1)S(1)} %add_convert_fusion.8), channel_id=1, source_target_pairs={{0,24},{1,25},{2,26},{3,27},{4,28},{5,29},{6,30},{7,31},{8,16},{9,... | collective-permute-start | bytes 110600 | tf_op jit(solution)/shard_map/ppermute | solution.py:384
  440.3 10.4 %collective-permute-start.29 = (bf16[24,768]{1,0:T(8,128)(2,1)S(1)}, bf16[24,768]{1,0:T(8,128)(2,1)S(1)}, u32[]{:S(2)}, u32[]{:S(2)}) collective-permute-start(bf16[24,768]{1,0:T(8,128)(2,1)S(1)} %add_convert_fusion.8), channel_id=1, source_target_pairs={{0,16},{1,17},{2,18},{3,19},{4,20},{5,21},{6,22},{7,23},{8,24},{9,... | collective-permute-start | bytes 110600 | tf_op jit(solution)/shard_map/ppermute | solution.py:384
  443.7 10.7 %collective-permute-start.30 = (bf16[24,768]{1,0:T(8,128)(2,1)S(1)}, bf16[24,768]{1,0:T(8,128)(2,1)S(1)}, u32[]{:S(2)}, u32[]{:S(2)}) collective-permute-start(bf16[24,768]{1,0:T(8,128)(2,1)S(1)} %add_convert_fusion.8), channel_id=1, source_target_pairs={{0,8},{1,9},{2,10},{3,11},{4,12},{5,13},{6,14},{7,15},{8,0},{9,1},... | collective-permute-start | bytes 110600 | tf_op jit(solution)/shard_map/ppermute | solution.py:384
  447.1 8.0 %collective-permute-start.65 = (f32[14,768]{1,0:T(8,128)S(1)}, f32[14,768]{1,0:T(8,128)S(1)}, u32[]{:S(2)}, u32[]{:S(2)}) collective-permute-start(f32[14,768]{1,0:T(8,128)S(1)} %fusion.26), channel_id=1, source_target_pairs={{0,4},{1,5},{2,6},{3,7},{4,0},{5,1},{6,2},{7,3},{8,12},{9,13},{10,... | collective-permute-start | bytes 129032 | tf_op jit(solution)/shard_map/ppermute | solution.py:384
  450.7 5.8 collective-permute-start.66
  458.6 6.1 %collective-permute-start.69 = (f32[14,768]{1,0:T(8,128)S(1)}, f32[14,768]{1,0:T(8,128)S(1)}, u32[]{:S(2)}, u32[]{:S(2)}) collective-permute-start(f32[14,768]{1,0:T(8,128)S(1)} %add_add_fusion.1), channel_id=1, source_target_pairs={{0,24},{1,25},{2,26},{3,27},{4,28},{5,29},{6,30},{7,31},{8,16},{9,... | collective-permute-start | bytes 129032 | tf_op jit(solution)/shard_map/ppermute | solution.py:384
  460.7 5.1 collective-permute-start.67
  463.2 5.4 collective-permute-start.32
  464.7 6.4 %collective-permute-start.31 = (bf16[96,768]{1,0:T(8,128)(2,1)}, bf16[96,768]{1,0:T(8,128)(2,1)}, u32[]{:S(2)}, u32[]{:S(2)}) collective-permute-start(bf16[96,768]{1,0:T(8,128)(2,1)} %pad_maximum_fusion.4), channel_id=1, source_target_pairs={{0,6},{1,7},{2,4},{3,5},{4,2},{5,3},{6,0},{7,1},{8,14},{9,15},{10,... | collective-permute-start | bytes 442376 | tf_op jit(solution)/shard_map/ppermute | solution.py:384
  465.8 6.1 %collective-permute-start.33 = (bf16[96,768]{1,0:T(8,128)(2,1)}, bf16[96,768]{1,0:T(8,128)(2,1)}, u32[]{:S(2)}, u32[]{:S(2)}) collective-permute-start(bf16[96,768]{1,0:T(8,128)(2,1)} %pad_maximum_fusion.4), channel_id=1, source_target_pairs={{0,4},{1,5},{2,6},{3,7},{4,0},{5,1},{6,2},{7,3},{8,12},{9,13},{10,... | collective-permute-start | bytes 442376 | tf_op jit(solution)/shard_map/ppermute | solution.py:384
  468.7 16.4 %collective-permute-start.49 = (bf16[384,768]{1,0:T(8,128)(2,1)}, bf16[384,768]{1,0:T(8,128)(2,1)S(1)}, u32[]{:S(2)}, u32[]{:S(2)}) collective-permute-start(bf16[384,768]{1,0:T(8,128)(2,1)} %dynamic-slice_convert_fusion.6), channel_id=1, source_target_pairs={{0,1},{1,0},{2,3},{3,2},{4,5},{5,4},{6,7},{7,6},{8,9},{9,8},{10,11... | collective-permute-start | bytes 1769480 | tf_op jit(solution)/shard_map/ppermute | solution.py:384
  474.6 6.1 %collective-permute-start.38 = (bf16[96,768]{1,0:T(8,128)(2,1)S(1)}, bf16[96,768]{1,0:T(8,128)(2,1)S(1)}, u32[]{:S(2)}, u32[]{:S(2)}) collective-permute-start(bf16[96,768]{1,0:T(8,128)(2,1)S(1)} %get-tuple-element.243), channel_id=1, source_target_pairs={{0,6},{1,7},{2,4},{3,5},{4,2},{5,3},{6,0},{7,1},{8,14},{9,15},{10,... | collective-permute-start | bytes 442376 | tf_op jit(solution)/shard_map/ppermute | solution.py:384
  476.1 6.1 %collective-permute-start.37 = (bf16[96,768]{1,0:T(8,128)(2,1)S(1)}, bf16[96,768]{1,0:T(8,128)(2,1)S(1)}, u32[]{:S(2)}, u32[]{:S(2)}) collective-permute-start(bf16[96,768]{1,0:T(8,128)(2,1)S(1)} %get-tuple-element.244), channel_id=1, source_target_pairs={{0,4},{1,5},{2,6},{3,7},{4,0},{5,1},{6,2},{7,3},{8,12},{9,13},{10,... | collective-permute-start | bytes 442376 | tf_op jit(solution)/shard_map/ppermute | solution.py:384
  477.5 5.1 collective-permute-start.36
  480.7 32.9 %collective-permute-start.34 = (bf16[384,768]{1,0:T(8,128)(2,1)S(1)}, bf16[384,768]{1,0:T(8,128)(2,1)S(1)}, u32[]{:S(2)}, u32[]{:S(2)}) collective-permute-start(bf16[384,768]{1,0:T(8,128)(2,1)S(1)} %pad_maximum_fusion.1), channel_id=1, source_target_pairs={{0,1},{1,0},{2,3},{3,2},{4,5},{5,4},{6,7},{7,6},{8,9},{9,8},{10,11... | collective-permute-start | bytes 1769480 | tf_op jit(solution)/shard_map/ppermute | solution.py:384
  482.8 5.9 collective-permute-start.41
  485.1 4.9 collective-permute-start.39
  490.0 5.8 collective-permute-start.42
  491.6 5.2 collective-permute-start.43
  495.8 6.1 %collective-permute-start.52 = (bf16[96,768]{1,0:T(8,128)(2,1)S(1)}, bf16[96,768]{1,0:T(8,128)(2,1)S(1)}, u32[]{:S(2)}, u32[]{:S(2)}) collective-permute-start(bf16[96,768]{1,0:T(8,128)(2,1)S(1)} %get-tuple-element.238), channel_id=1, source_target_pairs={{0,6},{1,7},{2,4},{3,5},{4,2},{5,3},{6,0},{7,1},{8,14},{9,15},{10,... | collective-permute-start | bytes 442376 | tf_op jit(solution)/shard_map/ppermute | solution.py:384
  496.8 5.8 collective-permute-start.51
  497.9 5.5 collective-permute-start.50
  503.5 5.9 collective-permute-start.55
  509.4 57.3 %collective-permute-start.23 = (bf16[1024,768]{1,0:T(8,128)(2,1)}, bf16[1024,768]{1,0:T(8,128)(2,1)}, u32[]{:S(2)}, u32[]{:S(2)}) collective-permute-start(bf16[1024,768]{1,0:T(8,128)(2,1)} %back_product.4), channel_id=1, source_target_pairs={{0,1},{1,0},{2,3},{3,2},{4,5},{5,4},{6,7},{7,6},{8,9},{9,8},{10,11... | collective-permute-start | bytes 4718600 | tf_op jit(solution)/shard_map/ppermute | solution.py:501
  510.1 9.9 %collective-permute-start.56 = (bf16[24,768]{1,0:T(8,128)(2,1)S(1)}, bf16[24,768]{1,0:T(8,128)(2,1)S(1)}, u32[]{:S(2)}, u32[]{:S(2)}) collective-permute-start(bf16[24,768]{1,0:T(8,128)(2,1)S(1)} %add_convert_fusion.6), channel_id=1, source_target_pairs={{0,24},{1,25},{2,26},{3,27},{4,28},{5,29},{6,30},{7,31},{8,16},{9,... | collective-permute-start | bytes 110600 | tf_op jit(solution)/shard_map/ppermute | solution.py:384
  512.4 8.7 %collective-permute-start.57 = (bf16[24,768]{1,0:T(8,128)(2,1)S(1)}, bf16[24,768]{1,0:T(8,128)(2,1)S(1)}, u32[]{:S(2)}, u32[]{:S(2)}) collective-permute-start(bf16[24,768]{1,0:T(8,128)(2,1)S(1)} %add_convert_fusion.6), channel_id=1, source_target_pairs={{0,16},{1,17},{2,18},{3,19},{4,20},{5,21},{6,22},{7,23},{8,24},{9,... | collective-permute-start | bytes 110600 | tf_op jit(solution)/shard_map/ppermute | solution.py:384
  513.7 9.1 %collective-permute-start.58 = (bf16[24,768]{1,0:T(8,128)(2,1)S(1)}, bf16[24,768]{1,0:T(8,128)(2,1)}, u32[]{:S(2)}, u32[]{:S(2)}) collective-permute-start(bf16[24,768]{1,0:T(8,128)(2,1)S(1)} %add_convert_fusion.6), channel_id=1, source_target_pairs={{0,8},{1,9},{2,10},{3,11},{4,12},{5,13},{6,14},{7,15},{8,0},{9,1},... | collective-permute-start | bytes 110600 | tf_op jit(solution)/shard_map/ppermute | solution.py:384
  520.0 8.3 %collective-permute-start.46 = (bf16[96,768]{1,0:T(8,128)(2,1)S(1)}, bf16[96,768]{1,0:T(8,128)(2,1)S(1)}, u32[]{:S(2)}, u32[]{:S(2)}) collective-permute-start(bf16[96,768]{1,0:T(8,128)(2,1)S(1)} %pad_maximum_fusion.5), channel_id=1, source_target_pairs={{0,2},{1,3},{2,0},{3,1},{4,6},{5,7},{6,4},{7,5},{8,10},{9,11},{10,... | collective-permute-start | bytes 442376 | tf_op jit(solution)/shard_map/ppermute | solution.py:384
  521.1 8.3 %collective-permute-start.45 = (bf16[96,768]{1,0:T(8,128)(2,1)S(1)}, bf16[96,768]{1,0:T(8,128)(2,1)S(1)}, u32[]{:S(2)}, u32[]{:S(2)}) collective-permute-start(bf16[96,768]{1,0:T(8,128)(2,1)S(1)} %pad_maximum_fusion.5), channel_id=1, source_target_pairs={{0,6},{1,7},{2,4},{3,5},{4,2},{5,3},{6,0},{7,1},{8,14},{9,15},{10,... | collective-permute-start | bytes 442376 | tf_op jit(solution)/shard_map/ppermute | solution.py:384
  522.7 7.7 %collective-permute-start.47 = (bf16[96,768]{1,0:T(8,128)(2,1)S(1)}, bf16[96,768]{1,0:T(8,128)(2,1)S(1)}, u32[]{:S(2)}, u32[]{:S(2)}) collective-permute-start(bf16[96,768]{1,0:T(8,128)(2,1)S(1)} %pad_maximum_fusion.5), channel_id=1, source_target_pairs={{0,4},{1,5},{2,6},{3,7},{4,0},{5,1},{6,2},{7,3},{8,12},{9,13},{10,... | collective-permute-start | bytes 442376 | tf_op jit(solution)/shard_map/ppermute | solution.py:384
  528.3 7.4 %collective-permute-start.60 = (bf16[96,768]{1,0:T(8,128)(2,1)S(1)}, bf16[96,768]{1,0:T(8,128)(2,1)S(1)}, u32[]{:S(2)}, u32[]{:S(2)}) collective-permute-start(bf16[96,768]{1,0:T(8,128)(2,1)S(1)} %pad_maximum_fusion.6), channel_id=1, source_target_pairs={{0,2},{1,3},{2,0},{3,1},{4,6},{5,7},{6,4},{7,5},{8,10},{9,11},{10,... | collective-permute-start | bytes 442376 | tf_op jit(solution)/shard_map/ppermute | solution.py:384
  529.3 6.5 %collective-permute-start.59 = (bf16[96,768]{1,0:T(8,128)(2,1)S(1)}, bf16[96,768]{1,0:T(8,128)(2,1)S(1)}, u32[]{:S(2)}, u32[]{:S(2)}) collective-permute-start(bf16[96,768]{1,0:T(8,128)(2,1)S(1)} %pad_maximum_fusion.6), channel_id=1, source_target_pairs={{0,6},{1,7},{2,4},{3,5},{4,2},{5,3},{6,0},{7,1},{8,14},{9,15},{10,... | collective-permute-start | bytes 442376 | tf_op jit(solution)/shard_map/ppermute | solution.py:384
  530.4 6.1 %collective-permute-start.61 = (bf16[96,768]{1,0:T(8,128)(2,1)S(1)}, bf16[96,768]{1,0:T(8,128)(2,1)S(1)}, u32[]{:S(2)}, u32[]{:S(2)}) collective-permute-start(bf16[96,768]{1,0:T(8,128)(2,1)S(1)} %pad_maximum_fusion.6), channel_id=1, source_target_pairs={{0,4},{1,5},{2,6},{3,7},{4,0},{5,1},{6,2},{7,3},{8,12},{9,13},{10,... | collective-permute-start | bytes 442376 | tf_op jit(solution)/shard_map/ppermute | solution.py:384
  538.3 9.0 %collective-permute-start.62 = (bf16[384,768]{1,0:T(8,128)(2,1)}, bf16[384,768]{1,0:T(8,128)(2,1)}, u32[]{:S(2)}, u32[]{:S(2)}) collective-permute-start(bf16[384,768]{1,0:T(8,128)(2,1)} %pad_maximum_fusion.3), channel_id=1, source_target_pairs={{0,1},{1,0},{2,3},{3,2},{4,5},{5,4},{6,7},{7,6},{8,9},{9,8},{10,11... | collective-permute-start | bytes 1769480 | tf_op jit(solution)/shard_map/ppermute | solution.py:384
  (72 other events, 551.1 us)
Sparse Core Ops, SparseCore 0:
  350.6 102.3 all-gather.2
